TPU v7x, 32 devices: a whole 2x2x4 slice. The times are simulated.
32 devices in a mesh: grp: 4 (over z), blk: 8 (over y, x, core).
Axes of the slice: x: 2, y: 2, z: 4, core: 2. Of those that a mesh axis runs over, the one named last changes fastest.
Arguments:
- embeddings: bfloat16 [4, 512, 1024], P('grp', 'blk'), may hold values from -72 to 72
- cluster_ids: int32 [4, 512], P('grp', 'blk'), may hold values from 0 to 15, never falling along the last dimension, each value on 1 to 128 neighbouring positions
- block_list: int32 [4, 64, 2], P('grp', 'blk'), may hold values from 0 to 7, as said below
- block_counts: int32 [4, 8], P('grp', 'blk'), may hold values from 1 to 8, as said below
- pair_targets: float32 [4, 64, 4096], P('grp', 'blk'), may hold values from -6 to 6
- w_left: bfloat16 [1024, 512], replicated, may hold values from -0.125 to 0.125
- w_right: bfloat16 [1024, 512], replicated, may hold values from -0.125 to 0.125
- hidden_bias: float32 [512], replicated, may hold values from -3 to 3
- w_middle: bfloat16 [512, 128], replicated, may hold values from -0.25 to 0.25
- w_final: float32 [128], replicated, may hold values from -0.5 to 0.5
Outputs:
- grad_embeddings: float32 [4, 512, 1024], P('grp', 'blk')
- grad_left: float32 [1024, 512], replicated
- grad_right: float32 [1024, 512], replicated
- grad_bias: float32 [512], replicated
- grad_middle: float32 [512, 128], replicated
- grad_final: float32 [128], replicated
Inputs may be any that keep to these rules, and one draw needn't show every extreme that they name: `block_list`: entries are panels of the device's own group; the column panel lies within one of the row panel. `block_counts`: slots of a device at and beyond its count are unused; in every group one device has exactly 8.
All inputs are finite; a program needn't handle non-finite values.
Results may differ from a plain program's by a relative error of at most 0.012.
Values may be sent and summed in bfloat16 or wider, within the bound.
A program may use at most 128 MiB of HBM per device.

v0:
```python
import math

import jax
import jax.numpy as jnp
from jax import lax
from jax.sharding import PartitionSpec as P

PANEL = 64
B_DEV = 8


def silu_slope(value):
    sigmoid_value = jax.nn.sigmoid(value)
    return sigmoid_value * (1.0 + value * (1.0 - sigmoid_value))


def pair_block(
    left_rows,
    right_rows,
    left_ids,
    right_ids,
    row_start,
    col_start,
    pair_target,
    hidden_bias,
    w_middle,
    w_final,
):
    panel_rows = left_rows.shape[0]
    hidden_width = left_rows.shape[1]
    pre_hidden = (
        left_rows.astype(jnp.float32)[:, None, :]
        + right_rows.astype(jnp.float32)[None, :, :]
        + hidden_bias
    )
    hidden = (
        jax.nn.silu(pre_hidden).astype(jnp.bfloat16).reshape(panel_rows * panel_rows, hidden_width)
    )
    pre_upper = jnp.dot(hidden, w_middle, preferred_element_type=jnp.float32)
    upper_act = jax.nn.silu(pre_upper)
    predicted = jnp.sum(upper_act * w_final, axis=1)
    left_pos = row_start + jnp.arange(panel_rows, dtype=jnp.int32)
    right_pos = col_start + jnp.arange(panel_rows, dtype=jnp.int32)
    same_cluster = (left_ids[:, None] == right_ids[None, :]) & (
        left_pos[:, None] != right_pos[None, :]
    )
    residual = jnp.where(same_cluster.reshape(-1), predicted - pair_target, 0.0)
    pair_slope = 16.0 * residual
    grad_final = jnp.sum(upper_act * pair_slope[:, None], axis=0)
    grad_second = (pair_slope[:, None] * w_final[None, :] * silu_slope(pre_upper)).astype(
        jnp.bfloat16
    )
    grad_middle = lax.dot_general(
        hidden, grad_second, (((0,), (0,)), ((), ())), preferred_element_type=jnp.float32
    )
    grad_hidden = lax.dot_general(
        grad_second, w_middle, (((1,), (1,)), ((), ())), preferred_element_type=jnp.float32
    )
    grad_first = grad_hidden.reshape(panel_rows, panel_rows, hidden_width) * silu_slope(pre_hidden)
    return (
        jnp.sum(grad_first, axis=1),
        jnp.sum(grad_first, axis=0),
        jnp.sum(grad_first, axis=(0, 1)),
        grad_middle,
        grad_final,
    )


def local(
    embeddings,
    cluster_ids,
    block_list,
    block_counts,
    pair_targets,
    w_left,
    w_right,
    hidden_bias,
    w_middle,
    w_final,
):
    local_emb = embeddings[0]
    local_left = jnp.dot(local_emb, w_left, preferred_element_type=jnp.float32).astype(jnp.bfloat16)
    local_right = jnp.dot(local_emb, w_right, preferred_element_type=jnp.float32).astype(
        jnp.bfloat16
    )
    left_all, right_all, group_ids = (
        lax.all_gather(local_left[None], "blk", axis=1, tiled=True),
        lax.all_gather(local_right[None], "blk", axis=1, tiled=True),
        lax.all_gather(cluster_ids, "blk", axis=1, tiled=True),
    )
    left_all = left_all[0]
    right_all = right_all[0]

    def fetch_panels(row_start, col_start):
        return (
            lax.dynamic_slice_in_dim(left_all, row_start, PANEL, 0),
            lax.dynamic_slice_in_dim(right_all, col_start, PANEL, 0),
        )

    group_ids = group_ids[0]
    local_blocks = block_list[0]
    local_targets = pair_targets[0]
    molecules = group_ids.shape[0]
    hidden_width = w_left.shape[1]

    def slot_step(slot, carry):
        part_left, part_right, sum_bias, sum_middle, sum_final = carry
        entry = lax.dynamic_index_in_dim(local_blocks, slot, 0, keepdims=False)
        row_start = entry[0] * PANEL
        col_start = entry[1] * PANEL
        pair_target = lax.dynamic_index_in_dim(local_targets, slot, 0, keepdims=False)
        left_rows, right_rows = fetch_panels(row_start, col_start)
        grad_rows, grad_cols, grad_bias, grad_middle, grad_final = pair_block(
            left_rows,
            right_rows,
            lax.dynamic_slice_in_dim(group_ids, row_start, PANEL, 0),
            lax.dynamic_slice_in_dim(group_ids, col_start, PANEL, 0),
            row_start,
            col_start,
            pair_target,
            hidden_bias,
            w_middle,
            w_final,
        )
        current = lax.dynamic_slice_in_dim(part_left, row_start, PANEL, 0)
        part_left = lax.dynamic_update_slice_in_dim(part_left, current + grad_rows, row_start, 0)
        current = lax.dynamic_slice_in_dim(part_right, col_start, PANEL, 0)
        part_right = lax.dynamic_update_slice_in_dim(part_right, current + grad_cols, col_start, 0)
        return (
            part_left,
            part_right,
            sum_bias + grad_bias,
            sum_middle + grad_middle,
            sum_final + grad_final,
        )

    empty = jnp.zeros((molecules, hidden_width), jnp.float32)
    start_state = (
        empty,
        empty,
        jnp.zeros((hidden_width,), jnp.float32),
        jnp.zeros(w_middle.shape, jnp.float32),
        jnp.zeros(w_final.shape, jnp.float32),
    )
    part_left, part_right, sum_bias, sum_middle, sum_final = lax.fori_loop(
        0, block_counts[0, 0], slot_step, start_state
    )
    rounded_left = part_left.astype(jnp.bfloat16)
    rounded_right = part_right.astype(jnp.bfloat16)
    own_left, own_right = (
        lax.psum_scatter(
            rounded_left.astype(jnp.float32).astype(jnp.bfloat16),
            "blk",
            scatter_dimension=0,
            tiled=True,
        ).astype(jnp.float32),
        lax.psum_scatter(
            rounded_right.astype(jnp.float32).astype(jnp.bfloat16),
            "blk",
            scatter_dimension=0,
            tiled=True,
        ).astype(jnp.float32),
    )
    left_grad = own_left.astype(jnp.bfloat16)
    right_grad = own_right.astype(jnp.bfloat16)
    grad_local = jnp.dot(left_grad, w_left.T, preferred_element_type=jnp.float32) + jnp.dot(
        right_grad, w_right.T, preferred_element_type=jnp.float32
    )
    weight_left = lax.dot_general(
        local_emb, left_grad, (((0,), (0,)), ((), ())), preferred_element_type=jnp.float32
    )
    weight_right = lax.dot_general(
        local_emb, right_grad, (((0,), (0,)), ((), ())), preferred_element_type=jnp.float32
    )
    summed = lax.psum((weight_left, weight_right, sum_bias, sum_middle, sum_final), ("grp", "blk"))
    devices = lax.axis_size("grp") * lax.axis_size("blk")
    scale = 1.0 / math.sqrt(devices * B_DEV * PANEL)
    return (
        grad_local[None],
        summed[0] * scale,
        summed[1] * scale,
        summed[2] * scale,
        summed[3] * scale,
        summed[4] * scale,
    )


def solution(mesh):
    return jax.shard_map(
        local,
        mesh=mesh,
        in_specs=(
            P("grp", "blk", None),
            P("grp", "blk"),
            P("grp", "blk", None),
            P("grp", "blk"),
            P("grp", "blk", None),
            P(),
            P(),
            P(),
            P(),
            P(),
        ),
        out_specs=(P("grp", "blk", None), P(), P(), P(), P(), P()),
        check_vma=False,
    )
```

profile of v0, /device:TPU:0, one launch (start us, length us, event | category | flops | bytes accessed | tf_op | source)
XLA Modules:
  0.0 514.2 jit_solution(3107231918358280894)
XLA Ops:
  9.6 12.4 %all-gather = bf16[512,512]{1,0:T(8,128)(2,1)} all-gather(bf16[64,512]{1,0:T(8,128)(2,1)S(1)} %convolution_convert_fusion.1), channel_id=2, replica_groups=mesh['grp'=4,'blk'=8] {'blk'}, dimensions={0}, use_global_device_ids=true | all-gather | bytes 589824 | tf_op jit(solution)/shard_map/all_gather | solution.py:87
  23.6 9.8 %all-gather.1 = bf16[512,512]{1,0:T(8,128)(2,1)S(1)} all-gather(bf16[64,512]{1,0:T(8,128)(2,1)S(1)} %convolution_convert_fusion), channel_id=3, replica_groups=mesh['grp'=4,'blk'=8] {'blk'}, dimensions={0}, use_global_device_ids=true | all-gather | bytes 589824 | tf_op jit(solution)/shard_map/all_gather | solution.py:88
  34.7 7.0 %all-reduce = s32[512]{0:T(512)S(1)} all-reduce(s32[512]{0:T(512)S(1)} %bitcast_dynamic-update-slice_fusion), channel_id=1, replica_groups=mesh['grp'=4,'blk'=8] {'blk'}, use_global_device_ids=true, to_apply=%add | all-reduce | flops 512 | bytes 4096 | tf_op jit(solution)/shard_map/squeeze | solution.py:100
  44.7 85.8 %while.18 = (s32[]{:T(128)}, f32[512,512]{1,0:T(8,128)}, f32[512,512]{1,0:T(8,128)}, f32[512]{0:T(512)S(1)}, f32[512,128]{1,0:T(8,128)}, /*index=5*/f32[128]{0:T...) while((s32[]{:T(128)}, f32[512,512]{1,0:T(8,128)}, ...), condition=%wide.region_6.7_spmd, body=%wide.region_0.6_spmd.sunk | while | flops 1688359040 | bytes 146592368 | solution.py:145
  49.6 3.4 multiply_convert_fusion.7
  56.9 5.3 %convolution_add_fusion.3 = f32[512,128]{1,0:T(8,128)} fusion(f32[512,128]{1,0:T(8,128)} %get-tuple-element.288, bf16[4096,512]{1,0:T(8,128)(2,1)} %copy-done.2, f32[4096,128]{1,0:T(8,128)S(1)} %get-tuple-element.254, f32[4096]{0:T(1024)S(1)} %select_multiply_fusion.2, f32[128]{0:T(128)S(1)} %get-tuple-element.317), kind=kOutput, calls=%fused_computation.11.clone.1 | convolution fusion | flops 542179328 | bytes 6832640 | tf_op jit(solution)/shard_map/while/body/dot_general | solution.py:53
  62.2 5.3 %multiply_reduce_fusion.7 = (f32[512]{0:T(512)S(1)}, f32[4096,512]{1,0:T(8,128)S(1)}) fusion(f32[64,64,512]{2,1,0:T(8,128)S(1)} %bitcast.64, f32[512]{0:T(512)S(1)} %get-tuple-element.315, bf16[512,128]{1,0:T(8,128)(2,1)S(1)} %copy-done.14, f32[4096,128]{1,0:T(8,128)S(1)} %get-tuple-element.254, f32[4096]{0:T(1024)S(1)} %select_multiply_fusion.2, ...), kind=kOutput, calls=%fused_computation.1.clone.1 | convolution fusion | flops 563084800 | bytes 19026432 | tf_op jit(solution)/shard_map/while/body/dot_general | solution.py:56
  67.5 3.9 fusion.36
  77.8 3.4 multiply_convert_fusion.7
  85.1 5.3 %convolution_add_fusion.3 = f32[512,128]{1,0:T(8,128)} fusion(f32[512,128]{1,0:T(8,128)} %get-tuple-element.288, bf16[4096,512]{1,0:T(8,128)(2,1)} %copy-done.2, f32[4096,128]{1,0:T(8,128)S(1)} %get-tuple-element.254, f32[4096]{0:T(1024)S(1)} %select_multiply_fusion.2, f32[128]{0:T(128)S(1)} %get-tuple-element.317), kind=kOutput, calls=%fused_computation.11.clone.1 | convolution fusion | flops 542179328 | bytes 6832640 | tf_op jit(solution)/shard_map/while/body/dot_general | solution.py:53
  90.4 5.3 %multiply_reduce_fusion.7 = (f32[512]{0:T(512)S(1)}, f32[4096,512]{1,0:T(8,128)S(1)}) fusion(f32[64,64,512]{2,1,0:T(8,128)S(1)} %bitcast.64, f32[512]{0:T(512)S(1)} %get-tuple-element.315, bf16[512,128]{1,0:T(8,128)(2,1)S(1)} %copy-done.14, f32[4096,128]{1,0:T(8,128)S(1)} %get-tuple-element.254, f32[4096]{0:T(1024)S(1)} %select_multiply_fusion.2, ...), kind=kOutput, calls=%fused_computation.1.clone.1 | convolution fusion | flops 563084800 | bytes 19026432 | tf_op jit(solution)/shard_map/while/body/dot_general | solution.py:56
  95.7 3.9 fusion.36
  106.1 3.4 multiply_convert_fusion.7
  113.4 5.3 %convolution_add_fusion.3 = f32[512,128]{1,0:T(8,128)} fusion(f32[512,128]{1,0:T(8,128)} %get-tuple-element.288, bf16[4096,512]{1,0:T(8,128)(2,1)} %copy-done.2, f32[4096,128]{1,0:T(8,128)S(1)} %get-tuple-element.254, f32[4096]{0:T(1024)S(1)} %select_multiply_fusion.2, f32[128]{0:T(128)S(1)} %get-tuple-element.317), kind=kOutput, calls=%fused_computation.11.clone.1 | convolution fusion | flops 542179328 | bytes 6832640 | tf_op jit(solution)/shard_map/while/body/dot_general | solution.py:53
  118.7 5.2 %multiply_reduce_fusion.7 = (f32[512]{0:T(512)S(1)}, f32[4096,512]{1,0:T(8,128)S(1)}) fusion(f32[64,64,512]{2,1,0:T(8,128)S(1)} %bitcast.64, f32[512]{0:T(512)S(1)} %get-tuple-element.315, bf16[512,128]{1,0:T(8,128)(2,1)S(1)} %copy-done.14, f32[4096,128]{1,0:T(8,128)S(1)} %get-tuple-element.254, f32[4096]{0:T(1024)S(1)} %select_multiply_fusion.2, ...), kind=kOutput, calls=%fused_computation.1.clone.1 | convolution fusion | flops 563084800 | bytes 19026432 | tf_op jit(solution)/shard_map/while/body/dot_general | solution.py:56
  123.9 3.9 fusion.36
  133.7 174.6 %reduce-scatter.5.cloned.1.call-done = bf16[64,512]{1,0:T(8,128)(2,1)} async-done(((bf16[512,512]{1,0:T(8,128)(2,1)}), bf16[64,512]{1,0:T(8,128)(2,1)}) %reduce-scatter.5.cloned.1.call-update) | async-done | bytes 65552 | tf_op jit(solution)/shard_map/reduce_scatter | solution.py:157
  308.4 2.6 convolution_bitcast_fusion
  311.0 35.5 %reduce-scatter.3.cloned.1.call-done = bf16[64,512]{1,0:T(8,128)(2,1)} async-done(((bf16[512,512]{1,0:T(8,128)(2,1)}), bf16[64,512]{1,0:T(8,128)(2,1)}) %reduce-scatter.3.cloned.1.call-update) | async-done | bytes 65552 | tf_op jit(solution)/shard_map/reduce_scatter | solution.py:151
  346.4 2.6 convolution_bitcast_fusion.1
  349.1 40.0 %all-reduce.1 = (f32[512]{0:T(512)S(1)}, f32[128]{0:T(128)S(1)}) all-reduce(f32[512]{0:T(512)S(1)} %get-tuple-element.90, f32[128]{0:T(128)S(1)} %get-tuple-element.92), channel_id=1, replica_groups=mesh['grp'=4,'blk'=8] {'grp','blk'}, use_global_device_ids=true, to_apply=%region_11.12 | all-reduce | flops 640 | bytes 5120 | tf_op jit(solution)/shard_map/psum | solution.py:175
  391.8 106.3 %all-reduce.5.cloned.1.call-done = (f32[1024,512]{0,1:T(8,128)}, f32[1024,512]{0,1:T(8,128)}, f32[512,128]{1,0:T(8,128)}) async-done(((f32[1024,512]{0,1:T(8,128)}, f32[1024,512]{0,1:T(8,128)}, f32[512,128]{1,0:T(8,128)}), (f32[1024,512]{0,1:T(8,128)}, f32[1024,512]{0,1:T(8,128)}, f32[512,128]{1,0:T(8,128)})) %all-reduce.5.cloned.1.call-update) | async-done | bytes 4456464 | tf_op jit(solution)/shard_map/psum | solution.py:175
  498.1 4.2 broadcast_multiply_fusion
  502.3 2.9 copy.16
  (150 shorter events, 40.8 us)
Async XLA Ops:
  7.2 26.2 %copy-start.17 = (u32[32]{0:T(128)S(1)}, u32[32]{0:T(128)}, u32[]{:S(2)}) copy-start(u32[32]{0:T(128)} %constant.49) | copy-start | bytes 388
  7.2 27.4 %copy-start.15 = (s32[1,64]{1,0:T(1,128)S(1)}, s32[1,64]{1,0:T(1,128)}, u32[]{:S(2)}) copy-start(s32[1,64]{1,0:T(1,128)} %param.13) | copy-start | bytes 772
  7.2 301.1 %reduce-scatter.5.cloned.1.call-start = ((), (), s32[]{:S(2)}) async-start(), calls=%async_computation.3 | async-start | bytes 589824 | tf_op jit(solution)/shard_map/reduce_scatter | solution.py:157
  22.0 22.7 %copy-start.11 = (f32[512]{0:T(512)S(1)}, f32[512]{0:T(512)}, u32[]{:S(2)}) copy-start(f32[512]{0:T(512)} %param.19) | copy-start | bytes 6148
  22.0 22.7 %copy-start.12 = (s32[1,8,2]{1,2,0:T(2,128)S(1)}, s32[1,8,2]{1,2,0:T(2,128)}, u32[]{:S(2)}) copy-start(s32[1,8,2]{1,2,0:T(2,128)} %param.14) | copy-start | bytes 196
  22.0 22.7 %copy-start.16 = (f32[128]{0:T(128)S(1)}, f32[128]{0:T(128)}, u32[]{:S(2)}) copy-start(f32[128]{0:T(128)} %param.21) | copy-start | bytes 1540
  56.1 6.0 %slice-start = ((s8[8388608]{0:T(1024)(128)(4,1)}), s8[4194304]{0:T(1024)(128)(4,1)S(1)}, s32[]{:S(2)}) async-start(s8[8388608]{0:T(1024)(128)(4,1)} %bitcast.63), calls=%async_computation.5 | async-start | bytes 8388608 | tf_op jit(solution)/shard_map/while
  56.9 5.3 %slice-start.1 = ((s8[8388608]{0:T(1024)(128)(4,1)}), s8[4194304]{0:T(1024)(128)(4,1)S(1)}, s32[]{:S(2)}) async-start(s8[8388608]{0:T(1024)(128)(4,1)} %bitcast.63), calls=%async_computation.6 | async-start | bytes 8388608 | tf_op jit(solution)/shard_map/while
  56.9 5.3 %copy-start.14 = (bf16[512,128]{1,0:T(8,128)(2,1)S(1)}, bf16[512,128]{1,0:T(8,128)(2,1)}, u32[]{:S(2)}) copy-start(bf16[512,128]{1,0:T(8,128)(2,1)} %get-tuple-element.316) | copy-start | bytes 393220 | tf_op jit(solution)/shard_map/while
  67.4 5.7 %copy-start.7 = (bf16[512,512]{1,0:T(8,128)(2,1)S(1)}, bf16[512,512]{1,0:T(8,128)(2,1)}, u32[]{:S(2)}) copy-start(bf16[512,512]{1,0:T(8,128)(2,1)} %copy-done.6) | copy-start | bytes 1572868 | tf_op jit(solution)/shard_map/while
  84.4 6.0 %slice-start = ((s8[8388608]{0:T(1024)(128)(4,1)}), s8[4194304]{0:T(1024)(128)(4,1)S(1)}, s32[]{:S(2)}) async-start(s8[8388608]{0:T(1024)(128)(4,1)} %bitcast.63), calls=%async_computation.5 | async-start | bytes 8388608 | tf_op jit(solution)/shard_map/while
  85.1 5.3 %slice-start.1 = ((s8[8388608]{0:T(1024)(128)(4,1)}), s8[4194304]{0:T(1024)(128)(4,1)S(1)}, s32[]{:S(2)}) async-start(s8[8388608]{0:T(1024)(128)(4,1)} %bitcast.63), calls=%async_computation.6 | async-start | bytes 8388608 | tf_op jit(solution)/shard_map/while
  85.1 5.3 %copy-start.14 = (bf16[512,128]{1,0:T(8,128)(2,1)S(1)}, bf16[512,128]{1,0:T(8,128)(2,1)}, u32[]{:S(2)}) copy-start(bf16[512,128]{1,0:T(8,128)(2,1)} %get-tuple-element.316) | copy-start | bytes 393220 | tf_op jit(solution)/shard_map/while
  95.7 5.7 %copy-start.7 = (bf16[512,512]{1,0:T(8,128)(2,1)S(1)}, bf16[512,512]{1,0:T(8,128)(2,1)}, u32[]{:S(2)}) copy-start(bf16[512,512]{1,0:T(8,128)(2,1)} %copy-done.6) | copy-start | bytes 1572868 | tf_op jit(solution)/shard_map/while
  112.6 6.0 %slice-start = ((s8[8388608]{0:T(1024)(128)(4,1)}), s8[4194304]{0:T(1024)(128)(4,1)S(1)}, s32[]{:S(2)}) async-start(s8[8388608]{0:T(1024)(128)(4,1)} %bitcast.63), calls=%async_computation.5 | async-start | bytes 8388608 | tf_op jit(solution)/shard_map/while
  113.4 5.3 %slice-start.1 = ((s8[8388608]{0:T(1024)(128)(4,1)}), s8[4194304]{0:T(1024)(128)(4,1)S(1)}, s32[]{:S(2)}) async-start(s8[8388608]{0:T(1024)(128)(4,1)} %bitcast.63), calls=%async_computation.6 | async-start | bytes 8388608 | tf_op jit(solution)/shard_map/while
  113.4 5.3 %copy-start.14 = (bf16[512,128]{1,0:T(8,128)(2,1)S(1)}, bf16[512,128]{1,0:T(8,128)(2,1)}, u32[]{:S(2)}) copy-start(bf16[512,128]{1,0:T(8,128)(2,1)} %get-tuple-element.316) | copy-start | bytes 393220 | tf_op jit(solution)/shard_map/while
  123.9 5.7 %copy-start.7 = (bf16[512,512]{1,0:T(8,128)(2,1)S(1)}, bf16[512,512]{1,0:T(8,128)(2,1)}, u32[]{:S(2)}) copy-start(bf16[512,512]{1,0:T(8,128)(2,1)} %copy-done.6) | copy-start | bytes 1572868 | tf_op jit(solution)/shard_map/while
  130.5 177.9 %copy-start.5 = (bf16[1,64,1024]{2,1,0:T(8,128)(2,1)S(1)}, bf16[1,64,1024]{2,1,0:T(8,128)(2,1)}, u32[]{:S(2)}) copy-start(bf16[1,64,1024]{2,1,0:T(8,128)(2,1)} %param.12) | copy-start | bytes 393220
  132.7 213.7 %reduce-scatter.3.cloned.1.call-start = ((), (), s32[]{:S(2)}) async-start(), calls=%async_computation.2 | async-start | bytes 589824 | tf_op jit(solution)/shard_map/reduce_scatter | solution.py:151
  133.7 364.4 %all-reduce.5.cloned.1.call-start = ((), (), s32[]{:S(2)}) async-start(), calls=%async_computation.4 | async-start | bytes 8912896 | tf_op jit(solution)/shard_map/psum | solution.py:175
  349.1 41.1 %copy-start.10 = (bf16[64,512]{1,0:T(8,128)(2,1)S(1)}, bf16[64,512]{1,0:T(8,128)(2,1)}, u32[]{:S(2)}) copy-start(bf16[64,512]{1,0:T(8,128)(2,1)} %reduce-scatter.3.cloned.1.call-done) | copy-start | bytes 196612
  349.1 41.5 %copy-start.4 = (bf16[1024,512]{1,0:T(8,128)(2,1)S(1)}, bf16[1024,512]{1,0:T(8,128)(2,1)}, u32[]{:S(2)}) copy-start(bf16[1024,512]{1,0:T(8,128)(2,1)} %param.18) | copy-start | bytes 3145732
  349.1 41.5 %copy-start.8 = (bf16[64,512]{1,0:T(8,128)(2,1)S(1)}, bf16[64,512]{1,0:T(8,128)(2,1)}, u32[]{:S(2)}) copy-start(bf16[64,512]{1,0:T(8,128)(2,1)} %reduce-scatter.5.cloned.1.call-done) | copy-start | bytes 196612
  (15 other events, 43.7 us)
Sparse Core Ops, SparseCore 0:
  132.8 175.4 reduce-scatter.4
  312.3 34.0 reduce-scatter.2
  353.0 144.9 all-reduce.4
where the time goes:
time: 516 us; the launch traced here: 514 us
  waiting for transfers between devices  316 us (61%)
  blocking collectives  69.1 us (13%)
  matrix products  45.2 us (9%)
  other arithmetic  44.6 us (9%)
  local copies, waits for them, and re-layouts  16.6 us (3%)
  between operations  14.5 us (3%)
  loops' own time  7.49 us (1%)
    reduce_scatter x1, waiting for transfers between devices, local(): lax.psum_scatter(rounded_right.astype(jnp.float32).astype(jnp.bfloat16),...  175 us
    psum x1, waiting for transfers between devices, local(): lax.psum((weight_left, weight_right, sum_bias, sum_middle, sum_final), ('...  106 us
    psum x1, blocking collectives, local(): lax.psum((weight_left, weight_right, sum_bias, sum_middle, sum_final), ('...  40 us
    reduce_scatter x1, waiting for transfers between devices, local(): lax.psum_scatter(rounded_left.astype(jnp.float32).astype(jnp.bfloat16), '...  35.5 us
    dot_general x3, matrix products, pair_block(): lax.dot_general(hidden, grad_second, (((0,), (0,)), ((), ())), preferred_...  15.8 us
    dot_general x3, matrix products, pair_block(): lax.dot_general(grad_second, w_middle, (((1,), (1,)), ((), ())), preferre...  15.8 us
    all_gather x1, blocking collectives, local(): lax.all_gather(local_left[None], 'blk', axis=1, tiled=True)  12.4 us
    reduce_sum x3, other arithmetic, pair_block(): jnp.sum(grad_first, axis=0)  11.8 us
  transfers between devices with their start and end apart: 3, of which 3 were waited for; matrix products, arithmetic and copies ran while one was open for 1% of the time, Pallas kernels for 0%

commit v1 on v0

v1 whole, which is shorter than its diff:
```python
import functools
import math

import jax
import jax.numpy as jnp
from jax import lax
from jax.experimental import pallas as pl
from jax.experimental.pallas import tpu as pltpu
from jax.sharding import PartitionSpec as P

ROWS = 16
COLS = 32
MESH = pl.DeviceIdType.MESH


def pair_kernel(
    left_ref, right_ref, bias_ref, row_ids_ref, col_ids_ref, target_ref, middle_ref, final_ref,
    left_out, right_out, sums_out,
    left_half, right_half, left_full, right_full, right_acc, row_acc, weight_row, target_row,
    half_middle, left_acc, final_acc,
):
    panel, hidden = left_ref.shape
    span = 3 * panel
    padded = right_acc.shape[0]
    upper = middle_ref.shape[1]
    fold = target_ref.shape[1] - 8
    middle_out = sums_out.at[0:upper, :]
    half_middle[...] = middle_ref[...] * jnp.bfloat16(0.5)
    left = left_ref[...].astype(jnp.float32)
    right = right_ref[...].astype(jnp.float32).reshape(span, hidden) + bias_ref[...]
    left_half[...] = 0.5 * left
    right_half[0:span, :] = 0.5 * right
    right_half[span:padded, :] = jnp.zeros((padded - span, hidden), jnp.float32)
    left_full[...] = left
    right_full[0:span, :] = right + 1.0
    right_full[span:padded, :] = jnp.zeros((padded - span, hidden), jnp.float32)
    right_acc[...] = jnp.zeros_like(right_acc)
    sums_out[...] = jnp.zeros_like(sums_out)
    final_acc[...] = jnp.zeros_like(final_acc)

    row_ids = row_ids_ref[...]
    col_ids = col_ids_ref[...].reshape(span, 128)[:, 0:panel]
    parts, numbers = [], []
    for offset in range(3):
        for lane in range(panel // fold):
            parts.append(target_ref[offset, 0:fold, lane * panel:(lane + 1) * panel])
        numbers.extend([target_ref[offset, fold:fold + 8, 0:panel]] * (panel // 8))
    col_pos = lax.broadcasted_iota(jnp.int32, (span, panel), 0) - panel
    row_pos = lax.broadcasted_iota(jnp.int32, (span, panel), 1)
    used = (col_ids == row_ids) & (col_pos != row_pos)
    counts = jnp.where(used, jnp.concatenate(numbers, axis=0), 0.0) * 16.0
    targets = jnp.where(used, jnp.concatenate(parts, axis=0), 0.0) * 16.0
    tiles = panel // ROWS
    active = jnp.where(counts > 0.0, 1.0, 0.0)
    for tile in range(tiles):
        weight_row[tile, 0:span, :] = counts[:, tile * ROWS:(tile + 1) * ROWS]
        weight_row[tile, span:padded, :] = jnp.zeros((padded - span, ROWS), jnp.float32)
        target_row[tile, 0:span, :] = targets[:, tile * ROWS:(tile + 1) * ROWS]
        target_row[tile, span:padded, :] = jnp.zeros((padded - span, ROWS), jnp.float32)

    where_col = (col_pos + panel).astype(jnp.float32)
    first_map = jnp.where(active > 0.0, where_col, float(padded))
    last_map = jnp.where(active > 0.0, where_col + 1.0, 0.0)
    half_final = 0.5 * final_ref[...]

    for tile in range(tiles):
        lanes = slice(tile * ROWS, (tile + 1) * ROWS)
        first = jnp.min(first_map[:, lanes]).astype(jnp.int32)
        last = jnp.max(last_map[:, lanes]).astype(jnp.int32)
        start = first // 8 * 8
        chunks = jnp.maximum(last - start + COLS - 1, 0) // COLS
        rows = slice(tile * ROWS, (tile + 1) * ROWS)
        row_acc[...] = jnp.zeros_like(row_acc)

        def chunk_step(step, carry):
            cols = pl.ds(pl.multiple_of(start + step * COLS, 8), COLS)
            pairs = ROWS * COLS
            half = left_half[rows, :][:, None, :] + right_half[cols, :][None, :, :]
            plus = left_full[rows, :][:, None, :] + right_full[cols, :][None, :, :]
            gate = 1.0 + jnp.tanh(half)
            act = half * gate
            slope = gate * (plus - act)
            act_low = act.astype(jnp.bfloat16).reshape(pairs, hidden)
            upper_half = jnp.dot(act_low, half_middle[...], preferred_element_type=jnp.float32)
            upper_gate = 1.0 + jnp.tanh(upper_half)
            upper_act = upper_half * upper_gate
            upper_slope = upper_gate * (1.0 + 2.0 * upper_half - upper_act)
            predicted = jnp.sum(upper_act * final_ref[...], axis=1, keepdims=True)
            weights = weight_row[tile, cols, :]
            goal = target_row[tile, cols, :]
            weights = jnp.concatenate([weights[:, a:a + 1] for a in range(ROWS)], axis=0)
            goal = jnp.concatenate([goal[:, a:a + 1] for a in range(ROWS)], axis=0)
            pair_slope = weights * predicted - goal
            final_acc[...] += jnp.sum(
                (upper_act * pair_slope).reshape(pairs // 8, 8, upper), axis=0
            )
            second = (pair_slope * half_final * upper_slope).astype(jnp.bfloat16)
            middle_out[...] += lax.dot_general(
                second, act_low, (((0,), (0,)), ((), ())), preferred_element_type=jnp.float32
            )
            back = lax.dot_general(
                second, half_middle[...], (((1,), (1,)), ((), ())),
                preferred_element_type=jnp.float32,
            )
            grad = back.reshape(ROWS, COLS, hidden) * slope
            row_acc[...] += jnp.sum(grad.reshape(ROWS, COLS // 8, 8, hidden), axis=1)
            right_acc[cols, :] += jnp.sum(grad, axis=0)
            return carry

        lax.fori_loop(0, chunks, chunk_step, 0)
        left_acc[rows, :] = jnp.sum(row_acc[...], axis=1)
    left_out[...] = left_acc[...].astype(jnp.bfloat16)
    sums_out[upper:upper + 1, :] = jnp.sum(left_acc[...], axis=0, keepdims=True)
    sums_out[upper + 1:upper + 2, 0:upper] = jnp.sum(final_acc[...], axis=0, keepdims=True)
    right_out[...] = right_acc[0:span, :].astype(jnp.bfloat16).reshape(3, panel, hidden)


def pair_grads(left, right, bias, row_ids, col_ids, targets, w_middle, w_final):
    panel, hidden = left.shape
    upper = w_middle.shape[1]
    span = 3 * panel
    padded = span + COLS
    f32 = jnp.float32
    return pl.pallas_call(
        pair_kernel,
        out_shape=(
            jax.ShapeDtypeStruct((panel, hidden), jnp.bfloat16),
            jax.ShapeDtypeStruct((3, panel, hidden), jnp.bfloat16),
            jax.ShapeDtypeStruct((upper + 8, hidden), f32),
        ),
        in_specs=[pl.BlockSpec(memory_space=pltpu.VMEM)] * 8,
        out_specs=[pl.BlockSpec(memory_space=pltpu.VMEM)] * 3,
        scratch_shapes=[
            pltpu.VMEM((panel, hidden), f32),
            pltpu.VMEM((padded, hidden), f32),
            pltpu.VMEM((panel, hidden), f32),
            pltpu.VMEM((padded, hidden), f32),
            pltpu.VMEM((padded, hidden), f32),
            pltpu.VMEM((ROWS, 8, hidden), f32),
            pltpu.VMEM((panel // ROWS, padded, ROWS), f32),
            pltpu.VMEM((panel // ROWS, padded, ROWS), f32),
            pltpu.VMEM((hidden, upper), jnp.bfloat16),
            pltpu.VMEM((panel, hidden), f32),
            pltpu.VMEM((8, upper), f32),
        ],
        compiler_params=pltpu.CompilerParams(vmem_limit_bytes=32 * 1024 * 1024),
        name="pair_grads",
    )(left, right, bias[None, :], row_ids, col_ids, targets, w_middle, w_final[None, :])


def reduce_kernel(
    n_grp, n_blk, scale,
    left_ref, right_ref, emb_ref, w_left_ref, w_right_ref,
    emb_out, final_out,
    edge, panels, partial, arrived, mine_g,
    edge_send, edge_recv, g_send, g_recv, gf_send, gf_recv,
    z_send, z_recv, a_send, a_recv, p_send, p_recv, q_send, q_recv,
):
    f32, bf16 = jnp.float32, jnp.bfloat16
    grp, blk = lax.axis_index("grp"), lax.axis_index("blk")
    chips = n_blk // 2
    chip, core = blk // 2, blk % 2
    panel, hidden = left_ref.shape
    width = hidden // n_grp
    twin = chip * 2 + 1 - core

    def copy(src, dst, send, recv, grp_to, blk_to):
        return pltpu.make_async_remote_copy(
            src_ref=src, dst_ref=dst, send_sem=send, recv_sem=recv,
            device_id=(grp_to, blk_to), device_id_type=MESH,
        )

    def plane(step):
        return lax.rem(chip + step, chips) * 2 + core

    def origin(step):
        return lax.rem(chip + chips - step, chips) * 2 + core

    barrier = pltpu.get_barrier_semaphore()

    def greet_blk(step, carry):
        pl.semaphore_signal(
            barrier, inc=1, device_id=(grp, lax.rem(blk + step, n_blk)), device_id_type=MESH
        )
        return carry

    def greet_grp(step, carry):
        pl.semaphore_signal(
            barrier, inc=1, device_id=(lax.rem(grp + step, n_grp), blk), device_id_type=MESH
        )
        return carry

    lax.fori_loop(1, n_blk, greet_blk, 0)
    lax.fori_loop(1, n_grp, greet_grp, 0)
    panels[0, blk] = left_ref[...]
    pl.semaphore_wait(barrier, n_blk - 1 + n_grp - 1)

    to_before = copy(
        right_ref.at[0], edge.at[1], edge_send.at[0], edge_recv.at[1], grp, lax.rem(blk + n_blk - 1, n_blk)
    )
    to_after = copy(
        right_ref.at[2], edge.at[0], edge_send.at[1], edge_recv.at[0], grp, lax.rem(blk + 1, n_blk)
    )
    to_before.start()
    to_after.start()

    def share(half):
        def send(step, carry):
            copy(
                panels.at[half, blk], panels.at[half, blk],
                g_send.at[half, step], g_recv.at[half, step], grp, plane(step),
            ).start()
            return carry
        lax.fori_loop(1, chips, send, 0)
        copy(
            panels.at[half, blk], panels.at[half, blk],
            gf_send.at[half, 0], gf_recv.at[half, 0], grp, twin,
        ).start()

    def forward(half):
        def hand(step, carry):
            slot = panels.at[half, origin(step)]
            copy(slot, slot, g_send.at[half, step], g_recv.at[half, step], grp, plane(step)).wait_recv()
            copy(slot, slot, gf_send.at[half, step], gf_recv.at[half, step], grp, twin).start()
            return carry
        lax.fori_loop(1, chips, hand, 0)

    def multiply(half):
        def take(step, carry):
            slot = panels.at[half, lax.rem(chip + chips - step, chips) * 2 + 1 - core]
            copy(slot, slot, gf_send.at[half, step], gf_recv.at[half, step], grp, twin).wait_recv()
            return carry
        lax.fori_loop(0, chips, take, 0)
        depth = emb_ref.shape[2]
        product = lax.dot_general(
            emb_ref[...].reshape(n_blk * panel, depth), panels[half].reshape(n_blk * panel, hidden),
            (((0,), (0,)), ((), ())), preferred_element_type=f32,
        )
        for part in range(n_grp):
            partial[half, part] = product[:, part * width:(part + 1) * width].astype(bf16)

        def send(step, carry):
            to = lax.rem(grp + step, n_grp)
            copy(
                partial.at[half, to], arrived.at[half, step],
                z_send.at[half, step], z_recv.at[half, step], to, blk,
            ).start()
            return carry
        lax.fori_loop(1, n_grp, send, 0)

    def spread(half, part):
        slot = final_out.at[half, blk, part]

        def send(step, carry):
            copy(
                slot, slot, p_send.at[half, part, step], p_recv.at[half, part, step], grp, plane(step)
            ).start()
            return carry
        lax.fori_loop(1, chips, send, 0)
        copy(slot, slot, q_send.at[half, part, 0], q_recv.at[half, part, 0], grp, twin).start()

    def combine(half):
        total = partial[half, grp].astype(f32)
        for step in range(1, n_grp):
            slot = arrived.at[half, step]
            copy(slot, slot, z_send.at[half, step], z_recv.at[half, step], grp, blk).wait_recv()
            total = total + arrived[half, step].astype(f32)
        final_out[half, blk, grp] = (total * scale).astype(bf16)
        slot = final_out.at[half, blk, grp]

        def send(step, carry):
            copy(
                slot, slot, a_send.at[half, step], a_recv.at[half, step],
                lax.rem(grp + step, n_grp), blk,
            ).start()
            return carry
        lax.fori_loop(1, n_grp, send, 0)
        spread(half, grp)

    share(0)
    to_before.wait_recv()
    to_after.wait_recv()
    right = right_ref[1].astype(f32)
    right = right + jnp.where(blk > 0, edge[0].astype(f32), 0.0)
    right = right + jnp.where(blk < n_blk - 1, edge[1].astype(f32), 0.0)
    panels[1, blk] = right.astype(bf16)
    mine_g[...] = right.astype(bf16)
    share(1)
    forward(0)
    emb_out[...] = lax.dot_general(
        left_ref[...], w_left_ref[...], (((1,), (1,)), ((), ())), preferred_element_type=f32
    )
    multiply(0)
    forward(1)
    emb_out[...] += lax.dot_general(
        mine_g[...], w_right_ref[...], (((1,), (1,)), ((), ())), preferred_element_type=f32
    )
    multiply(1)
    combine(0)
    combine(1)
    for half in range(2):
        def pass_on(step, carry):
            part = lax.rem(grp + n_grp - step, n_grp)
            slot = final_out.at[half, blk, part]
            copy(slot, slot, a_send.at[half, step], a_recv.at[half, step], grp, blk).wait_recv()
            spread(half, part)
            return carry
        lax.fori_loop(1, n_grp, pass_on, 0)

    def hand_on(index, carry):
        half, rest = index // n_grp, lax.rem(index, n_grp)
        part = lax.rem(grp + n_grp - rest, n_grp)

        def hand(step, inner):
            slot = final_out.at[half, origin(step), part]
            copy(
                slot, slot, p_send.at[half, part, step], p_recv.at[half, part, step], grp, plane(step)
            ).wait_recv()
            copy(
                slot, slot, q_send.at[half, part, step], q_recv.at[half, part, step], grp, twin
            ).start()
            return inner
        return lax.fori_loop(1, chips, hand, carry)
    lax.fori_loop(0, 2 * n_grp, hand_on, 0)

    def finish(index, carry):
        half, part = index // n_grp, lax.rem(index, n_grp)

        def end(step, inner):
            slot = final_out.at[half, lax.rem(chip + chips - step, chips) * 2 + 1 - core, part]
            copy(
                slot, slot, q_send.at[half, part, step], q_recv.at[half, part, step], grp, twin
            ).wait()
            return inner
        lax.fori_loop(0, chips, end, 0)

        def sent(step, inner):
            slot = final_out.at[half, blk, part]
            copy(
                slot, slot, p_send.at[half, part, step], p_recv.at[half, part, step], grp, plane(step)
            ).wait_send()
            return inner
        return lax.fori_loop(1, chips, sent, carry)
    lax.fori_loop(0, 2 * n_grp, finish, 0)

    to_before.wait_send()
    to_after.wait_send()
    for half in range(2):
        def g_done(step, carry):
            slot = panels.at[half, blk]
            copy(slot, slot, g_send.at[half, step], g_recv.at[half, step], grp, plane(step)).wait_send()
            return carry
        lax.fori_loop(1, chips, g_done, 0)

        def gf_done(step, carry):
            slot = panels.at[half, blk]
            copy(slot, slot, gf_send.at[half, step], gf_recv.at[half, step], grp, twin).wait_send()
            return carry
        lax.fori_loop(0, chips, gf_done, 0)

        def z_done(step, carry):
            slot = partial.at[half, 0]
            copy(slot, slot, z_send.at[half, step], z_recv.at[half, step], grp, blk).wait_send()
            slot = final_out.at[half, blk, 0]
            copy(slot, slot, a_send.at[half, step], a_recv.at[half, step], grp, blk).wait_send()
            return carry
        lax.fori_loop(1, n_grp, z_done, 0)


def reduce_grads(n_grp, n_blk, scale, left_grad, right_part, emb_cols, w_left, w_right):
    panel, hidden = left_grad.shape
    depth = emb_cols.shape[2]
    wide = w_left.shape[0]
    chips = n_blk // 2
    width = hidden // n_grp
    bf16 = jnp.bfloat16
    dma = pltpu.SemaphoreType.DMA
    return pl.pallas_call(
        functools.partial(reduce_kernel, n_grp, n_blk, scale),
        out_shape=(
            jax.ShapeDtypeStruct((panel, wide), jnp.float32),
            jax.ShapeDtypeStruct((2, n_blk, n_grp, depth, width), bf16),
        ),
        in_specs=[pl.BlockSpec(memory_space=pltpu.VMEM)] * 5,
        out_specs=[pl.BlockSpec(memory_space=pltpu.VMEM)] * 2,
        scratch_shapes=[
            pltpu.VMEM((2, panel, hidden), bf16),
            pltpu.VMEM((2, n_blk, panel, hidden), bf16),
            pltpu.VMEM((2, n_grp, depth, width), bf16),
            pltpu.VMEM((2, n_grp, depth, width), bf16),
            pltpu.VMEM((panel, hidden), bf16),
            dma((2,)), dma((2,)),
            dma((2, chips)), dma((2, chips)), dma((2, chips)), dma((2, chips)),
            dma((2, n_grp)), dma((2, n_grp)), dma((2, n_grp)), dma((2, n_grp)),
            dma((2, n_grp, chips)), dma((2, n_grp, chips)),
            dma((2, n_grp, chips)), dma((2, n_grp, chips)),
        ],
        compiler_params=pltpu.CompilerParams(
            collective_id=1, has_side_effects=True, vmem_limit_bytes=40 * 1024 * 1024
        ),
        name="reduce_grads",
    )(left_grad, right_part, emb_cols, w_left, w_right)


def gather_kernel(
    n_blk,
    emb_ref, w_left_ref, w_right_ref, ids_ref, target_ref, block_ref, count_ref,
    left_out, right_out, ids_out, target_out, emb_out,
    emb_cols, ids_mine, target_mine, target_in,
    e_send, e_recv, t_send, t_recv, r_send, r_recv, i_send, i_recv,
):
    f32, bf16 = jnp.float32, jnp.bfloat16
    grp, blk = lax.axis_index("grp"), lax.axis_index("blk")
    depth = emb_out.shape[2]
    slots, fold, lanes = target_ref.shape
    before, after = lax.rem(blk + n_blk - 1, n_blk), lax.rem(blk + 1, n_blk)

    def copy(src, dst, send, recv, blk_to):
        return pltpu.make_async_remote_copy(
            src_ref=src, dst_ref=dst, send_sem=send, recv_sem=recv,
            device_id=(grp, blk_to), device_id_type=MESH,
        )

    barrier = pltpu.get_barrier_semaphore()

    def greet(step, carry):
        pl.semaphore_signal(
            barrier, inc=1, device_id=(grp, lax.rem(blk + step, n_blk)), device_id_type=MESH
        )
        return carry
    lax.fori_loop(1, n_blk, greet, 0)

    for to in range(n_blk):
        emb_cols[to] = emb_ref[:, to * depth:(to + 1) * depth]
    ids_mine[...] = jnp.broadcast_to(ids_ref[...], ids_mine.shape)
    ids_out[1] = ids_mine[...]

    def sum_pair(index, carry):
        to, offset = index // 3, lax.rem(index, 3)
        total = jnp.zeros((fold, lanes), f32)
        number = jnp.zeros((8, lanes), f32)
        for slot in range(slots):
            row, col = block_ref[slot, 0], block_ref[slot, 1]
            hit = (row == to) & (col - row == offset - 1) & (slot < count_ref[0, 0])
            weight = jnp.where(hit, 1.0, 0.0).astype(f32)
            total = total + weight * target_ref[slot]
            number = number + weight
        target_mine[to, offset, 0:fold, :] = total
        target_mine[to, offset, fold:fold + 8, :] = number
        return carry
    lax.fori_loop(0, 3 * n_blk, sum_pair, 0)
    pl.semaphore_wait(barrier, n_blk - 1)

    right_out[1] = jnp.dot(
        emb_ref[...], w_right_ref[...], preferred_element_type=f32
    ).astype(bf16)
    exchanges = [
        copy(right_out.at[1], right_out.at[2], r_send.at[0], r_recv.at[0], before),
        copy(right_out.at[1], right_out.at[0], r_send.at[1], r_recv.at[1], after),
        copy(ids_mine, ids_out.at[2], i_send.at[0], i_recv.at[0], before),
        copy(ids_mine, ids_out.at[0], i_send.at[1], i_recv.at[1], after),
    ]
    for exchange in exchanges:
        exchange.start()

    def send_targets(step, carry):
        to = lax.rem(blk + step, n_blk)
        copy(target_mine.at[to], target_in.at[step], t_send.at[step], t_recv.at[step], to).start()
        return carry
    lax.fori_loop(1, n_blk, send_targets, 0)

    def send_emb(step, carry):
        to = lax.rem(blk + step, n_blk)
        copy(emb_cols.at[to], emb_out.at[blk], e_send.at[step], e_recv.at[step], to).start()
        return carry
    lax.fori_loop(1, n_blk, send_emb, 0)

    left_out[...] = jnp.dot(emb_ref[...], w_left_ref[...], preferred_element_type=f32).astype(bf16)
    emb_out[blk] = emb_cols[blk]
    target_out[...] = target_mine[blk]

    def take_targets(step, carry):
        slot = target_in.at[step]
        copy(slot, slot, t_send.at[step], t_recv.at[step], blk).wait_recv()
        target_out[...] += target_in[step]
        return carry
    lax.fori_loop(1, n_blk, take_targets, 0)

    def finish(step, carry):
        slot = emb_out.at[lax.rem(blk + n_blk - step, n_blk)]
        copy(slot, slot, e_send.at[step], e_recv.at[step], blk).wait()
        copy(target_mine.at[0], target_in.at[0], t_send.at[step], t_recv.at[step], blk).wait_send()
        return carry
    lax.fori_loop(1, n_blk, finish, 0)
    for exchange in exchanges:
        exchange.wait()


def gather_panels(n_blk, emb, w_left, w_right, ids, targets, blocks, counts):
    f32, bf16 = jnp.float32, jnp.bfloat16
    panel, wide = emb.shape
    hidden = w_left.shape[1]
    fold, lanes = targets.shape[1:]
    depth = wide // n_blk
    dma = pltpu.SemaphoreType.DMA
    vmem, smem = pl.BlockSpec(memory_space=pltpu.VMEM), pl.BlockSpec(memory_space=pltpu.SMEM)
    return pl.pallas_call(
        functools.partial(gather_kernel, n_blk),
        out_shape=(
            jax.ShapeDtypeStruct((panel, hidden), bf16),
            jax.ShapeDtypeStruct((3, panel, hidden), bf16),
            jax.ShapeDtypeStruct((3, panel, 128), f32),
            jax.ShapeDtypeStruct((3, fold + 8, lanes), f32),
            jax.ShapeDtypeStruct((n_blk, panel, depth), bf16),
        ),
        in_specs=[vmem] * 5 + [smem] * 2,
        out_specs=[vmem] * 5,
        scratch_shapes=[
            pltpu.VMEM((n_blk, panel, depth), bf16),
            pltpu.VMEM((panel, 128), f32),
            pltpu.VMEM((n_blk, 3, fold + 8, lanes), f32),
            pltpu.VMEM((n_blk, 3, fold + 8, lanes), f32),
            dma((n_blk,)), dma((n_blk,)), dma((n_blk,)), dma((n_blk,)),
            dma((2,)), dma((2,)), dma((2,)), dma((2,)),
        ],
        compiler_params=pltpu.CompilerParams(
            collective_id=2, has_side_effects=True, vmem_limit_bytes=32 * 1024 * 1024
        ),
        name="gather_panels",
    )(emb, w_left, w_right, ids, targets, blocks, counts)


def local(
    embeddings, cluster_ids, block_list, block_counts, pair_targets,
    w_left, w_right, hidden_bias, w_middle, w_final,
):
    f32, bf16 = jnp.float32, jnp.bfloat16
    n_blk = lax.axis_size("blk")
    n_grp = lax.axis_size("grp")
    emb = embeddings[0]
    panel = emb.shape[0]
    slots = block_list.shape[1]
    hidden = w_left.shape[1]
    upper = w_middle.shape[1]
    fold = panel * panel // 128
    targets = pair_targets[0].reshape(slots, panel, panel // fold, fold)
    targets = targets.transpose(0, 3, 2, 1).reshape(slots, fold, 128)
    ids = cluster_ids[0].astype(f32)
    left, right, col_ids, targets, emb_cols = gather_panels(
        n_blk, emb, w_left, w_right, ids[:, None], targets, block_list[0], block_counts
    )
    left_grad, right_part, sums = pair_grads(
        left, right, hidden_bias, ids[None, :], col_ids, targets, w_middle, w_final
    )
    scale = 1.0 / math.sqrt(n_grp * n_blk * slots * panel)
    grad_local, weight = reduce_grads(
        n_grp, n_blk, scale, left_grad, right_part, emb_cols, w_left, w_right
    )
    sums = lax.psum(sums, ("grp", "blk")) * scale
    weight = weight.astype(f32).transpose(0, 1, 3, 2, 4).reshape(2, emb.shape[1], hidden)
    return (
        grad_local[None],
        weight[0],
        weight[1],
        sums[upper],
        sums[:upper].T,
        sums[upper + 1, :upper],
    )


def solution(mesh):
    return jax.shard_map(
        local,
        mesh=mesh,
        in_specs=(
            P("grp", "blk", None), P("grp", "blk"), P("grp", "blk", None), P("grp", "blk"),
            P("grp", "blk", None), P(), P(), P(), P(), P(),
        ),
        out_specs=(P("grp", "blk", None), P(), P(), P(), P(), P()),
        check_vma=False,
    )
```

time: 516 us -> 191 us (0.37)
  waiting for transfers between devices: 316 us -> 88.6 us
  Pallas kernels: 0 us -> 72.4 us
  blocking collectives: 69.1 us -> 0 us
  matrix products: 45.2 us -> 0 us
  other arithmetic: 44.6 us -> 2.15 us
  loops' own time: 7.49 us -> 0 us
    reduce_scatter x2 -> x0, waiting for transfers between devices: 210 us -> none  [the longest x1 175 us: local(): lax.psum_scatter(rounded_right.astype(jnp.float32).astype(jnp.bfloat16),...]
    pallas_call x0 -> x3, Pallas kernels: none -> 72.4 us  [the longest x1 40.5 us: reduce_grads(): pl.pallas_call(functools.partial(reduce_kernel, n_grp, n_blk, scale), out...]
    dot_general x15 -> x0, matrix products: 45.2 us -> none  [the longest x3 15.8 us: pair_block(): lax.dot_general(hidden, grad_second, (((0,), (0,)), ((), ())), preferred_...]
    psum x1 -> x0, blocking collectives: 40 us -> none  [local(): lax.psum((weight_left, weight_right, sum_bias, sum_middle, sum_final), ('...]
    all_gather x2 -> x0, blocking collectives: 22.1 us -> none  [the longest x1 12.4 us: local(): lax.all_gather(local_left[None], 'blk', axis=1, tiled=True)]
    psum x1, waiting for transfers between devices: 106 us -> 88.6 us  [local(): sums = lax.psum(sums, ('grp', 'blk')) * scale]
    convert_element_type x11 -> x1, other arithmetic: 15.8 us -> 0.66 us  [local(): ids = cluster_ids[0].astype(f32)]
    reduce_sum x6 -> x0, other arithmetic: 14 us -> none  [the longest x3 11.8 us: pair_block(): jnp.sum(grad_first, axis=0)]
  transfers between devices with their start and end apart: 3 -> 1, of which waited for: 3 -> 1; matrix products, arithmetic and copies ran while one was open for 1% -> 3% of each run, Pallas kernels for 0% -> 21%
where the time goes in v1:
time: 191 us
  waiting for transfers between devices  88.6 us (46%)
  Pallas kernels  72.4 us (38%)
  between operations  14.9 us (8%)
  local copies, waits for them, and re-layouts  13.1 us (7%)
  other arithmetic  2.15 us (1%)
    psum x1, waiting for transfers between devices, local(): sums = lax.psum(sums, ('grp', 'blk')) * scale  88.6 us
    pallas_call x1, Pallas kernels, reduce_grads(): pl.pallas_call(functools.partial(reduce_kernel, n_grp, n_blk, scale), out...  40.5 us
    pallas_call x1, Pallas kernels, pair_grads(): pl.pallas_call(pair_kernel, out_shape=(jax.ShapeDtypeStruct((panel, hidde...  16.5 us
    pallas_call x1, Pallas kernels, gather_panels(): pl.pallas_call(functools.partial(gather_kernel, n_blk), out_shape=(jax.Sh...  15.4 us
    unnamed x19, local copies, waits for them, and re-layouts  8.85 us
  transfers between devices with their start and end apart: 1, of which 1 were waited for; matrix products, arithmetic and copies ran while one was open for 3% of the time, Pallas kernels for 21%

profile of v1, /device:TPU:0, one launch (start us, length us, event | category | flops | bytes accessed | tf_op | source)
XLA Modules:
  0.0 191.1 jit_solution(3260880221893133263)
XLA Ops:
  7.2 0.0 all-reduce.2.cloned.1.call-start
  7.9 0.7 fusion.1
  8.6 0.8 copy.22.block_ref
  9.4 0.1 copy.21.ids_ref
  9.5 1.4 reshape_squeeze.3
  10.9 0.2 copy.20
  11.1 0.2 reshape.31.target_ref
  11.3 1.2 copy-done.1
  12.5 0.9 copy-done.4
  13.4 15.4 %gather_panels.1 = (bf16[64,512]{1,0:T(8,128)(2,1)S(1)}, bf16[3,64,512]{2,1,0:T(8,128)(2,1)S(1)}, f32[3,64,128]{2,1,0:T(8,128)S(1)}, f32[3,40,128]{2,1,0:T(8,128)S(1)}, bf16[8,64,128]{2,1,0:T(8,128)(2,1)S(1)}) custom-call(bf16[64,1024]{1,0:T(8,128)(2,1)S(1)} %bitcast.24, bf16[1024,512]{1,0:T(8,128)(2,1)S(1)} %copy-done, bf16[1024,512]{1,0:T(8,128)(2,1)S(1)} %copy-done.1, ...), custom_call_target="tpu_custom_call" | custom-call | tf_op jit(solution)/shard_map/gather_panels/pallas_call | solution.py:507
  28.8 16.5 %pair_grads.1 = (bf16[64,512]{1,0:T(8,128)(2,1)S(1)}, bf16[3,64,512]{2,1,0:T(8,128)(2,1)S(1)}, f32[136,512]{1,0:T(8,128)}) custom-call(bf16[64,512]{1,0:T(8,128)(2,1)S(1)} %get-tuple-element.16.left_ref, bf16[3,64,512]{2,1,0:T(8,128)(2,1)S(1)} %get-tuple-element.17.right_ref, f32[1,512]{1,0:T(1,128)S(1)} %bitcast.25, ...), custom_call_target="tpu_custom_call" | custom-call | tf_op jit(solution)/shard_map/pair_grads/pallas_call | solution.py:124
  45.3 0.0 all-reduce.2.cloned.1.call-update
  45.4 40.5 %reduce_grads.1 = (f32[64,1024]{1,0:T(8,128)S(1)}, bf16[2,8,4,128,128]{4,3,2,1,0:T(8,128)(2,1)S(1)}) custom-call(bf16[64,512]{1,0:T(8,128)(2,1)S(1)} %get-tuple-element.20.left_ref, bf16[3,64,512]{2,1,0:T(8,128)(2,1)S(1)} %get-tuple-element.21.right_ref, bf16[8,64,128]{2,1,0:T(8,128)(2,1)S(1)} %get-tuple-element.22.emb_ref, bf16[1024,512]{1,0:T(8,128)(2,1)S(1)} %copy-done, ...), custom_call_target="tpu_custom_call" | custom-call | tf_op jit(solution)/shard_map/reduce_grads/pallas_call | solution.py:378
  85.9 0.5 convert_bitcast_fusion
  86.4 0.5 fusion
  86.9 1.4 copy.29
  88.2 1.4 copy.28
  89.6 2.5 %copy_bitcast_fusion = (f32[1024,512]{1,0:T(8,128)}, f32[1024,512]{1,0:T(8,128)}) fusion(f32[128,8,4,128]{3,2,1,0:T(4,128)S(1)} %bitcast.27, f32[128,8,4,128]{3,2,1,0:T(4,128)S(1)} %bitcast.28), kind=kLoop, calls=%fused_computation.1 | loop fusion | bytes 8388608
  92.0 88.6 %all-reduce.2.cloned.1.call-done = f32[136,512]{1,0:T(8,128)} async-done(((f32[136,512]{1,0:T(8,128)}), f32[136,512]{1,0:T(8,128)}) %all-reduce.2.cloned.1.call-update) | async-done | bytes 278544 | tf_op jit(solution)/shard_map/psum | solution.py:559
  180.6 1.0 broadcast_multiply_fusion
  181.6 0.5 slice_bitcast_fusion.1
  182.1 0.6 slice.24
  182.7 0.8 copy.27
  183.5 0.7 copy.39
  (13 shorter events, 0.0 us)
Async XLA Ops:
  7.2 4.1 %copy-start = (bf16[1024,512]{1,0:T(8,128)(2,1)S(1)}, bf16[1024,512]{1,0:T(8,128)(2,1)}, u32[]{:S(2)}) copy-start(bf16[1024,512]{1,0:T(8,128)(2,1)} %w_left_ref.3) | copy-start | bytes 3145732
  7.2 173.4 %all-reduce.2.cloned.1.call-start = ((), (), s32[]{:S(2)}) async-start(), calls=%async_computation | async-start | bytes 557056 | tf_op jit(solution)/shard_map/psum | solution.py:559
  9.5 19.3 %copy-start.3 = (bf16[512,128]{1,0:T(8,128)(2,1)S(1)}, bf16[512,128]{1,0:T(8,128)(2,1)}, u32[]{:S(2)}) copy-start(bf16[512,128]{1,0:T(8,128)(2,1)} %middle_ref.1) | copy-start | bytes 393220
  9.5 19.4 %copy-start.5 = (f32[512]{0:T(512)S(1)}, f32[512]{0:T(512)}, u32[]{:S(2)}) copy-start(f32[512]{0:T(512)} %param.17) | copy-start | bytes 6148
  9.5 19.4 %copy-start.6 = (f32[128]{0:T(128)S(1)}, f32[128]{0:T(128)}, u32[]{:S(2)}) copy-start(f32[128]{0:T(128)} %param.19) | copy-start | bytes 1540
  11.3 1.2 copy-start.1
  12.5 0.9 copy-start.4
  13.4 32.0 %copy-start.2 = (bf16[1024,512]{1,0:T(8,128)(2,1)S(1)}, bf16[1024,512]{1,0:T(8,128)(2,1)}, u32[]{:S(2)}) copy-start(bf16[1024,512]{1,0:T(8,128)(2,1)} %w_right_ref.3) | copy-start | bytes 3145732
Sparse Core Ops, SparseCore 0:
  45.5 135.0 all-reduce.1

commit v2 on v1

--- a/solution.py
+++ b/solution.py
@@ -9,7 +9,7 @@
 from jax.sharding import PartitionSpec as P
 
 ROWS = 16
-COLS = 32
+COLS = 48
 MESH = pl.DeviceIdType.MESH
 
 
@@ -17,14 +17,13 @@
     left_ref, right_ref, bias_ref, row_ids_ref, col_ids_ref, target_ref, middle_ref, final_ref,
     left_out, right_out, sums_out,
     left_half, right_half, left_full, right_full, right_acc, row_acc, weight_row, target_row,
-    half_middle, left_acc, final_acc,
+    half_middle, left_acc, final_acc, middle_acc,
 ):
     panel, hidden = left_ref.shape
     span = 3 * panel
     padded = right_acc.shape[0]
     upper = middle_ref.shape[1]
     fold = target_ref.shape[1] - 8
-    middle_out = sums_out.at[0:upper, :]
     half_middle[...] = middle_ref[...] * jnp.bfloat16(0.5)
     left = left_ref[...].astype(jnp.float32)
     right = right_ref[...].astype(jnp.float32).reshape(span, hidden) + bias_ref[...]
@@ -35,7 +34,7 @@
     right_full[0:span, :] = right + 1.0
     right_full[span:padded, :] = jnp.zeros((padded - span, hidden), jnp.float32)
     right_acc[...] = jnp.zeros_like(right_acc)
-    sums_out[...] = jnp.zeros_like(sums_out)
+    middle_acc[...] = jnp.zeros_like(middle_acc)
     final_acc[...] = jnp.zeros_like(final_acc)
 
     row_ids = row_ids_ref[...]
@@ -95,7 +94,7 @@
                 (upper_act * pair_slope).reshape(pairs // 8, 8, upper), axis=0
             )
             second = (pair_slope * half_final * upper_slope).astype(jnp.bfloat16)
-            middle_out[...] += lax.dot_general(
+            middle_acc[...] += lax.dot_general(
                 second, act_low, (((0,), (0,)), ((), ())), preferred_element_type=jnp.float32
             )
             back = lax.dot_general(
@@ -110,8 +109,12 @@
         lax.fori_loop(0, chunks, chunk_step, 0)
         left_acc[rows, :] = jnp.sum(row_acc[...], axis=1)
     left_out[...] = left_acc[...].astype(jnp.bfloat16)
-    sums_out[upper:upper + 1, :] = jnp.sum(left_acc[...], axis=0, keepdims=True)
-    sums_out[upper + 1:upper + 2, 0:upper] = jnp.sum(final_acc[...], axis=0, keepdims=True)
+    sums_out[0:upper, :] = middle_acc[...].astype(jnp.bfloat16)
+    bias_row = jnp.sum(left_acc[...], axis=0, keepdims=True)
+    final_row = jnp.sum(final_acc[...], axis=0, keepdims=True)
+    final_row = jnp.concatenate([final_row] * (hidden // upper), axis=1)
+    row_at = lax.broadcasted_iota(jnp.int32, (16, hidden), 0)
+    sums_out[upper:upper + 16, :] = jnp.where(row_at == 0, bias_row, final_row).astype(jnp.bfloat16)
     right_out[...] = right_acc[0:span, :].astype(jnp.bfloat16).reshape(3, panel, hidden)
 
 
@@ -126,7 +129,7 @@
         out_shape=(
             jax.ShapeDtypeStruct((panel, hidden), jnp.bfloat16),
             jax.ShapeDtypeStruct((3, panel, hidden), jnp.bfloat16),
-            jax.ShapeDtypeStruct((upper + 8, hidden), f32),
+            jax.ShapeDtypeStruct((upper + 16, hidden), jnp.bfloat16),
         ),
         in_specs=[pl.BlockSpec(memory_space=pltpu.VMEM)] * 8,
         out_specs=[pl.BlockSpec(memory_space=pltpu.VMEM)] * 3,
@@ -142,6 +145,7 @@
             pltpu.VMEM((hidden, upper), jnp.bfloat16),
             pltpu.VMEM((panel, hidden), f32),
             pltpu.VMEM((8, upper), f32),
+            pltpu.VMEM((upper, hidden), f32),
         ],
         compiler_params=pltpu.CompilerParams(vmem_limit_bytes=32 * 1024 * 1024),
         name="pair_grads",
@@ -150,11 +154,12 @@
 
 def reduce_kernel(
     n_grp, n_blk, scale,
-    left_ref, right_ref, emb_ref, w_left_ref, w_right_ref,
-    emb_out, final_out,
-    edge, panels, partial, arrived, mine_g,
+    left_ref, right_ref, emb_ref, w_left_ref, w_right_ref, sums_ref,
+    emb_out, final_out, small_out,
+    edge, panels, partial, arrived, mine_g, small, small_in, small_z,
     edge_send, edge_recv, g_send, g_recv, gf_send, gf_recv,
     z_send, z_recv, a_send, a_recv, p_send, p_recv, q_send, q_recv,
+    s_send, s_recv, sz_send, sz_recv, sa_send, sa_recv,
 ):
     f32, bf16 = jnp.float32, jnp.bfloat16
     grp, blk = lax.axis_index("grp"), lax.axis_index("blk")
@@ -193,6 +198,15 @@
     lax.fori_loop(1, n_blk, greet_blk, 0)
     lax.fori_loop(1, n_grp, greet_grp, 0)
     panels[0, blk] = left_ref[...]
+    share_of = small.shape[1]
+    deep = sums_ref.shape[0] // 16
+    for tile in range(n_blk * share_of):
+        at = small.at[tile // share_of, tile % share_of]
+        if tile < deep * (hidden // 128):
+            down, across = tile % deep, tile // deep
+            at[...] = sums_ref[down * 16:(down + 1) * 16, across * 128:(across + 1) * 128]
+        else:
+            at[...] = jnp.zeros((16, 128), bf16)
     pl.semaphore_wait(barrier, n_blk - 1 + n_grp - 1)
 
     to_before = copy(
@@ -278,6 +292,12 @@
         spread(half, grp)
 
     share(0)
+
+    def small_start(step, carry):
+        to = lax.rem(blk + step, n_blk)
+        copy(small.at[to], small_in.at[step], s_send.at[step], s_recv.at[step], grp, to).start()
+        return carry
+    lax.fori_loop(1, n_blk, small_start, 0)
     to_before.wait_recv()
     to_after.wait_recv()
     right = right_ref[1].astype(f32)
@@ -291,12 +311,42 @@
         left_ref[...], w_left_ref[...], (((1,), (1,)), ((), ())), preferred_element_type=f32
     )
     multiply(0)
+    small_sum = small[blk].astype(f32)
+    for step in range(1, n_blk):
+        slot = small_in.at[step]
+        copy(slot, slot, s_send.at[step], s_recv.at[step], grp, blk).wait_recv()
+        small_sum = small_sum + small_in[step].astype(f32)
+    small_z[grp] = small_sum.astype(bf16)
+
+    def small_across(step, carry):
+        slot = small_z.at[grp]
+        copy(slot, slot, sz_send.at[step], sz_recv.at[step], lax.rem(grp + step, n_grp), blk).start()
+        return carry
+    lax.fori_loop(1, n_grp, small_across, 0)
     forward(1)
     emb_out[...] += lax.dot_general(
         mine_g[...], w_right_ref[...], (((1,), (1,)), ((), ())), preferred_element_type=f32
     )
     multiply(1)
     combine(0)
+
+    def small_take(step, carry):
+        slot = small_z.at[lax.rem(grp + n_grp - step, n_grp)]
+        copy(slot, slot, sz_send.at[step], sz_recv.at[step], grp, blk).wait_recv()
+        return carry
+    lax.fori_loop(1, n_grp, small_take, 0)
+    small_total = small_z[0].astype(f32)
+    for group in range(1, n_grp):
+        small_total = small_total + small_z[group].astype(f32)
+    small_out[blk] = small_total.astype(bf16)
+
+    def small_spread(step, carry):
+        slot = small_out.at[blk]
+        copy(
+            slot, slot, sa_send.at[step], sa_recv.at[step], grp, lax.rem(blk + step, n_blk)
+        ).start()
+        return carry
+    lax.fori_loop(1, n_blk, small_spread, 0)
     combine(1)
     for half in range(2):
         def pass_on(step, carry):
@@ -345,6 +395,19 @@
 
     to_before.wait_send()
     to_after.wait_send()
+
+    def small_end(step, carry):
+        slot = small_out.at[lax.rem(blk + n_blk - step, n_blk)]
+        copy(slot, slot, sa_send.at[step], sa_recv.at[step], grp, blk).wait()
+        copy(small.at[0], small_in.at[0], s_send.at[step], s_recv.at[step], grp, blk).wait_send()
+        return carry
+    lax.fori_loop(1, n_blk, small_end, 0)
+
+    def small_end_z(step, carry):
+        slot = small_z.at[0]
+        copy(slot, slot, sz_send.at[step], sz_recv.at[step], grp, blk).wait_send()
+        return carry
+    lax.fori_loop(1, n_grp, small_end_z, 0)
     for half in range(2):
         def g_done(step, carry):
             slot = panels.at[half, blk]
@@ -367,12 +430,13 @@
         lax.fori_loop(1, n_grp, z_done, 0)
 
 
-def reduce_grads(n_grp, n_blk, scale, left_grad, right_part, emb_cols, w_left, w_right):
+def reduce_grads(n_grp, n_blk, scale, left_grad, right_part, emb_cols, w_left, w_right, sums):
     panel, hidden = left_grad.shape
     depth = emb_cols.shape[2]
     wide = w_left.shape[0]
     chips = n_blk // 2
     width = hidden // n_grp
+    share_of = -(-(sums.shape[0] // 16 * (hidden // 128)) // n_blk)
     bf16 = jnp.bfloat16
     dma = pltpu.SemaphoreType.DMA
     return pl.pallas_call(
@@ -380,33 +444,98 @@
         out_shape=(
             jax.ShapeDtypeStruct((panel, wide), jnp.float32),
             jax.ShapeDtypeStruct((2, n_blk, n_grp, depth, width), bf16),
+            jax.ShapeDtypeStruct((n_blk, share_of, 16, 128), bf16),
         ),
-        in_specs=[pl.BlockSpec(memory_space=pltpu.VMEM)] * 5,
-        out_specs=[pl.BlockSpec(memory_space=pltpu.VMEM)] * 2,
+        in_specs=[pl.BlockSpec(memory_space=pltpu.VMEM)] * 6,
+        out_specs=[pl.BlockSpec(memory_space=pltpu.VMEM)] * 3,
         scratch_shapes=[
             pltpu.VMEM((2, panel, hidden), bf16),
             pltpu.VMEM((2, n_blk, panel, hidden), bf16),
             pltpu.VMEM((2, n_grp, depth, width), bf16),
             pltpu.VMEM((2, n_grp, depth, width), bf16),
             pltpu.VMEM((panel, hidden), bf16),
+            pltpu.VMEM((n_blk, share_of, 16, 128), bf16),
+            pltpu.VMEM((n_blk, share_of, 16, 128), bf16),
+            pltpu.VMEM((n_grp, share_of, 16, 128), bf16),
             dma((2,)), dma((2,)),
             dma((2, chips)), dma((2, chips)), dma((2, chips)), dma((2, chips)),
             dma((2, n_grp)), dma((2, n_grp)), dma((2, n_grp)), dma((2, n_grp)),
             dma((2, n_grp, chips)), dma((2, n_grp, chips)),
             dma((2, n_grp, chips)), dma((2, n_grp, chips)),
+            dma((n_blk,)), dma((n_blk,)), dma((n_grp,)), dma((n_grp,)), dma((n_blk,)), dma((n_blk,)),
         ],
         compiler_params=pltpu.CompilerParams(
             collective_id=1, has_side_effects=True, vmem_limit_bytes=40 * 1024 * 1024
         ),
         name="reduce_grads",
-    )(left_grad, right_part, emb_cols, w_left, w_right)
+    )(left_grad, right_part, emb_cols, w_left, w_right, sums)
+
+
+def unpack_kernel(scale, pieces_ref, small_ref, left_out, right_out, bias_out, middle_out, final_out):
+    f32 = jnp.float32
+    blocks, n_grp, depth, width = pieces_ref.shape[1:]
+    for half, out in enumerate((left_out, right_out)):
+        for block in range(blocks):
+            for part in range(n_grp):
+                out[block * depth:(block + 1) * depth, part * width:(part + 1) * width] = (
+                    pieces_ref[half, block, part].astype(f32)
+                )
+
+    @pl.when(pl.program_id(0) == 0)
+    def _():
+        share_of = small_ref.shape[1]
+        upper = middle_out.shape[1]
+        deep = upper // 16 + 1
+
+        def tile(down, across):
+            at = across * deep + down
+            return small_ref[at // share_of, at % share_of].astype(f32) * scale
+
+        for across in range(middle_out.shape[0] // 128):
+            lanes = slice(across * 128, (across + 1) * 128)
+            rows = jnp.concatenate([tile(down, across) for down in range(deep - 1)], axis=0)
+            middle_out[lanes, :] = rows.T
+            bias_out[:, lanes] = tile(deep - 1, across)[0:1, :]
+        final_out[...] = tile(deep - 1, 0)[1:2, 0:upper]
+
+
+def unpack_grads(scale, pieces, small, hidden, upper):
+    _, n_blk, n_grp, depth, width = pieces.shape
+    steps = math.gcd(n_blk, 4)
+    blocks = n_blk // steps
+    f32 = jnp.float32
+    rows = blocks * depth
+    return pl.pallas_call(
+        functools.partial(unpack_kernel, scale),
+        grid=(steps,),
+        out_shape=(
+            jax.ShapeDtypeStruct((n_blk * depth, hidden), f32),
+            jax.ShapeDtypeStruct((n_blk * depth, hidden), f32),
+            jax.ShapeDtypeStruct((1, hidden), f32),
+            jax.ShapeDtypeStruct((hidden, upper), f32),
+            jax.ShapeDtypeStruct((1, upper), f32),
+        ),
+        in_specs=[
+            pl.BlockSpec((2, blocks, n_grp, depth, width), lambda i: (0, i, 0, 0, 0)),
+            pl.BlockSpec(small.shape, lambda i: (0, 0, 0, 0)),
+        ],
+        out_specs=[
+            pl.BlockSpec((rows, hidden), lambda i: (i, 0)),
+            pl.BlockSpec((rows, hidden), lambda i: (i, 0)),
+            pl.BlockSpec((1, hidden), lambda i: (0, 0)),
+            pl.BlockSpec((hidden, upper), lambda i: (0, 0)),
+            pl.BlockSpec((1, upper), lambda i: (0, 0)),
+        ],
+        compiler_params=pltpu.CompilerParams(vmem_limit_bytes=24 * 1024 * 1024),
+        name="unpack_grads",
+    )(pieces, small)
 
 
 def gather_kernel(
     n_blk,
     emb_ref, w_left_ref, w_right_ref, ids_ref, target_ref, block_ref, count_ref,
     left_out, right_out, ids_out, target_out, emb_out,
-    emb_cols, ids_mine, target_mine, target_in,
+    emb_cols, ids_mine, target_mine, target_in, w_both, w_sem,
     e_send, e_recv, t_send, t_recv, r_send, r_recv, i_send, i_recv,
 ):
     f32, bf16 = jnp.float32, jnp.bfloat16
@@ -421,6 +550,10 @@
             device_id=(grp, blk_to), device_id_type=MESH,
         )
 
+    fetch_right = pltpu.make_async_copy(w_right_ref, w_both.at[1], w_sem.at[1])
+    fetch_left = pltpu.make_async_copy(w_left_ref, w_both.at[0], w_sem.at[0])
+    fetch_right.start()
+    fetch_left.start()
     barrier = pltpu.get_barrier_semaphore()
 
     def greet(step, carry):
@@ -451,8 +584,14 @@
     lax.fori_loop(0, 3 * n_blk, sum_pair, 0)
     pl.semaphore_wait(barrier, n_blk - 1)
 
+    def send_targets(step, carry):
+        to = lax.rem(blk + step, n_blk)
+        copy(target_mine.at[to], target_in.at[step], t_send.at[step], t_recv.at[step], to).start()
+        return carry
+    lax.fori_loop(1, n_blk, send_targets, 0)
+    fetch_right.wait()
     right_out[1] = jnp.dot(
-        emb_ref[...], w_right_ref[...], preferred_element_type=f32
+        emb_ref[...], w_both[1], preferred_element_type=f32
     ).astype(bf16)
     exchanges = [
         copy(right_out.at[1], right_out.at[2], r_send.at[0], r_recv.at[0], before),
@@ -463,19 +602,14 @@
     for exchange in exchanges:
         exchange.start()
 
-    def send_targets(step, carry):
-        to = lax.rem(blk + step, n_blk)
-        copy(target_mine.at[to], target_in.at[step], t_send.at[step], t_recv.at[step], to).start()
-        return carry
-    lax.fori_loop(1, n_blk, send_targets, 0)
-
     def send_emb(step, carry):
         to = lax.rem(blk + step, n_blk)
         copy(emb_cols.at[to], emb_out.at[blk], e_send.at[step], e_recv.at[step], to).start()
         return carry
     lax.fori_loop(1, n_blk, send_emb, 0)
 
-    left_out[...] = jnp.dot(emb_ref[...], w_left_ref[...], preferred_element_type=f32).astype(bf16)
+    fetch_left.wait()
+    left_out[...] = jnp.dot(emb_ref[...], w_both[0], preferred_element_type=f32).astype(bf16)
     emb_out[blk] = emb_cols[blk]
     target_out[...] = target_mine[blk]
 
@@ -503,6 +637,7 @@
     fold, lanes = targets.shape[1:]
     depth = wide // n_blk
     dma = pltpu.SemaphoreType.DMA
+    hbm = pl.BlockSpec(memory_space=pl.ANY)
     vmem, smem = pl.BlockSpec(memory_space=pltpu.VMEM), pl.BlockSpec(memory_space=pltpu.SMEM)
     return pl.pallas_call(
         functools.partial(gather_kernel, n_blk),
@@ -513,13 +648,15 @@
             jax.ShapeDtypeStruct((3, fold + 8, lanes), f32),
             jax.ShapeDtypeStruct((n_blk, panel, depth), bf16),
         ),
-        in_specs=[vmem] * 5 + [smem] * 2,
+        in_specs=[vmem, hbm, hbm, vmem, vmem, smem, smem],
         out_specs=[vmem] * 5,
         scratch_shapes=[
             pltpu.VMEM((n_blk, panel, depth), bf16),
             pltpu.VMEM((panel, 128), f32),
             pltpu.VMEM((n_blk, 3, fold + 8, lanes), f32),
             pltpu.VMEM((n_blk, 3, fold + 8, lanes), f32),
+            pltpu.VMEM((2, wide, hidden), bf16),
+            dma((2,)),
             dma((n_blk,)), dma((n_blk,)), dma((n_blk,)), dma((n_blk,)),
             dma((2,)), dma((2,)), dma((2,)), dma((2,)),
         ],
@@ -553,19 +690,13 @@
         left, right, hidden_bias, ids[None, :], col_ids, targets, w_middle, w_final
     )
     scale = 1.0 / math.sqrt(n_grp * n_blk * slots * panel)
-    grad_local, weight = reduce_grads(
-        n_grp, n_blk, scale, left_grad, right_part, emb_cols, w_left, w_right
-    )
-    sums = lax.psum(sums, ("grp", "blk")) * scale
-    weight = weight.astype(f32).transpose(0, 1, 3, 2, 4).reshape(2, emb.shape[1], hidden)
-    return (
-        grad_local[None],
-        weight[0],
-        weight[1],
-        sums[upper],
-        sums[:upper].T,
-        sums[upper + 1, :upper],
-    )
+    grad_local, pieces, small = reduce_grads(
+        n_grp, n_blk, scale, left_grad, right_part, emb_cols, w_left, w_right, sums
+    )
+    grad_left, grad_right, grad_bias, grad_middle, grad_final = unpack_grads(
+        scale, pieces, small, hidden, upper
+    )
+    return grad_local[None], grad_left, grad_right, grad_bias[0], grad_middle, grad_final[0]
 
 
 def solution(mesh):

time: 191 us -> 86.1 us (0.45)
  waiting for transfers between devices: 88.6 us -> 0 us
  between operations: 14.9 us -> 1.47 us
  local copies, waits for them, and re-layouts: 13.1 us -> 5.48 us
  Pallas kernels: 72.4 us -> 77.4 us
    psum x1 -> x0, waiting for transfers between devices: 88.6 us -> none  [local(): sums = lax.psum(sums, ('grp', 'blk')) * scale]
    pallas_call x1, Pallas kernels: 40.5 us -> 46.6 us  [reduce_grads(): pl.pallas_call(functools.partial(reduce_kernel, n_grp, n_blk, scale), out...]
    unnamed x19 -> x15, local copies, waits for them, and re-layouts: 8.85 us -> 2.85 us
    pallas_call x1, Pallas kernels: 16.5 us -> 12.7 us  [pair_grads(): pl.pallas_call(pair_kernel, out_shape=(jax.ShapeDtypeStruct((panel, hidde...]
    pallas_call x0 -> x1, Pallas kernels: none -> 2.85 us  [unpack_grads(): pl.pallas_call(functools.partial(unpack_kernel, scale), grid=(steps,), ou...]
  transfers between devices with their start and end apart: 1 -> 0, of which waited for: 1 -> 0; matrix products, arithmetic and copies ran while one was open for 3% -> 0% of each run, Pallas kernels for 21% -> 0%
where the time goes in v2:
time: 86.1 us; the launch traced here: 85 us
  Pallas kernels  77.4 us (90%)
  local copies, waits for them, and re-layouts  5.48 us (6%)
  between operations  1.47 us (2%)
    pallas_call x1, Pallas kernels, reduce_grads(): pl.pallas_call(functools.partial(reduce_kernel, n_grp, n_blk, scale), out...  46.6 us
    pallas_call x1, Pallas kernels, gather_panels(): pl.pallas_call(functools.partial(gather_kernel, n_blk), out_shape=(jax.Sh...  15.3 us
    pallas_call x1, Pallas kernels, pair_grads(): pl.pallas_call(pair_kernel, out_shape=(jax.ShapeDtypeStruct((panel, hidde...  12.7 us
    unnamed x15, local copies, waits for them, and re-layouts  2.85 us
    pallas_call x1, Pallas kernels, unpack_grads(): pl.pallas_call(functools.partial(unpack_kernel, scale), grid=(steps,), ou...  2.85 us

profile of v2, /device:TPU:0, one launch (start us, length us, event | category | flops | bytes accessed | tf_op | source)
XLA Modules:
  0.0 85.0 jit_solution(6646111815817884077)
XLA Ops:
  0.6 0.0 copy-start
  1.4 0.7 fusion
  2.0 0.8 copy.21.block_ref
  2.8 0.1 copy.20.ids_ref
  2.9 0.0 copy-start.3
  2.9 0.0 copy-start.5
  2.9 0.0 copy-start.6
  2.9 1.4 %reshape_squeeze.3 = f32[8,64,2,32]{3,2,1,0:T(2,128)S(1)} reshape(f32[1,8,4096]{2,1,0:T(8,128)} %param.14) | data formatting | bytes 262144 | tf_op jit(solution)/shard_map/reshape;squeeze | solution.py:683
  4.3 0.2 copy.19
  4.5 0.2 reshape.26.target_ref
  4.7 0.0 copy-done
  4.7 0.0 copy-start.1
  4.7 1.2 %copy-done.1 = bf16[1024,512]{1,0:T(8,128)(2,1)S(1)} copy-done((bf16[1024,512]{1,0:T(8,128)(2,1)S(1)}, bf16[1024,512]{1,0:T(8,128)(2,1)}, u32[]{:S(2)}) %copy-start.1) | copy-done | bytes 1048600
  5.9 0.0 copy-start.4
  5.9 0.9 %copy-done.4 = bf16[1,64,1024]{2,1,0:T(8,128)(2,1)S(1)} copy-done((bf16[1,64,1024]{2,1,0:T(8,128)(2,1)S(1)}, bf16[1,64,1024]{2,1,0:T(8,128)(2,1)}, u32[]{:S(2)}) %copy-start.4) | copy-done | bytes 131096
  6.8 15.3 %gather_panels.1 = (bf16[64,512]{1,0:T(8,128)(2,1)S(1)}, bf16[3,64,512]{2,1,0:T(8,128)(2,1)S(1)}, f32[3,64,128]{2,1,0:T(8,128)S(1)}, f32[3,40,128]{2,1,0:T(8,128)S(1)}, bf16[8,64,128]{2,1,0:T(8,128)(2,1)S(1)}) custom-call(bf16[64,1024]{1,0:T(8,128)(2,1)S(1)} %bitcast.11, bf16[1024,512]{1,0:T(8,128)(2,1)S(1)} %copy-done, bf16[1024,512]{1,0:T(8,128)(2,1)S(1)} %copy-done.1, ...), custom_call_target="tpu_custom_call" | custom-call | tf_op jit(solution)/shard_map/gather_panels/pallas_call | solution.py:642
  22.1 0.0 copy-done.3
  22.1 0.0 copy-done.5
  22.2 0.0 copy-done.6
  22.2 12.7 %pair_grads.1 = (bf16[64,512]{1,0:T(8,128)(2,1)S(1)}, bf16[3,64,512]{2,1,0:T(8,128)(2,1)S(1)}, bf16[144,512]{1,0:T(8,128)(2,1)S(1)}) custom-call(bf16[64,512]{1,0:T(8,128)(2,1)S(1)} %get-tuple-element.22.left_ref, bf16[3,64,512]{2,1,0:T(8,128)(2,1)S(1)} %get-tuple-element.23.right_ref, f32[1,512]{1,0:T(1,128)S(1)} %bitcast.12, ...), custom_call_target="tpu_custom_call" | custom-call | tf_op jit(solution)/shard_map/pair_grads/pallas_call | solution.py:127
  34.8 0.0 copy-done.2
  34.9 46.6 %reduce_grads.1 = (f32[64,1024]{1,0:T(8,128)S(1)}, bf16[2,8,4,128,128]{4,3,2,1,0:T(8,128)(2,1)S(1)}, bf16[8,5,16,128]{3,2,1,0:T(8,128)(2,1)S(1)}) custom-call(bf16[64,512]{1,0:T(8,128)(2,1)S(1)} %get-tuple-element.26.left_ref, bf16[3,64,512]{2,1,0:T(8,128)(2,1)S(1)} %get-tuple-element.27.right_ref, bf16[8,64,128]{2,1,0:T(8,128)(2,1)S(1)} %get-tuple-element.28.emb_ref, ...), custom_call_target="tpu_custom_call" | custom-call | tf_op jit(solution)/shard_map/reduce_grads/pallas_call | solution.py:442
  81.5 2.8 %unpack_grads.1 = (f32[1024,512]{1,0:T(8,128)}, f32[1024,512]{1,0:T(8,128)}, f32[1,512]{1,0:T(1,128)}, f32[512,128]{1,0:T(8,128)}, f32[1,128]{1,0:T(1,128)}) custom-call(bf16[2,8,4,128,128]{4,3,2,1,0:T(8,128)(2,1)S(1)} %get-tuple-element.31.pieces_ref, bf16[8,5,16,128]{3,2,1,0:T(8,128)(2,1)S(1)} %get-tuple-element.32.small_ref), custom_call_target="tpu_custom_call" | custom-call | tf_op jit(solution)/shard_map/unpack_grads/pallas_call | solution.py:508
  84.3 0.7 copy.24
  (1 shorter events, 0.0 us)
Async XLA Ops:
  0.6 4.1 %copy-start = (bf16[1024,512]{1,0:T(8,128)(2,1)S(1)}, bf16[1024,512]{1,0:T(8,128)(2,1)}, u32[]{:S(2)}) copy-start(bf16[1024,512]{1,0:T(8,128)(2,1)} %w_left_ref.3) | copy-start | bytes 3145732
  2.9 19.3 %copy-start.3 = (bf16[512,128]{1,0:T(8,128)(2,1)S(1)}, bf16[512,128]{1,0:T(8,128)(2,1)}, u32[]{:S(2)}) copy-start(bf16[512,128]{1,0:T(8,128)(2,1)} %middle_ref.1) | copy-start | bytes 393220
  2.9 19.3 %copy-start.5 = (f32[512]{0:T(512)S(1)}, f32[512]{0:T(512)}, u32[]{:S(2)}) copy-start(f32[512]{0:T(512)} %param.17) | copy-start | bytes 6148
  2.9 19.3 %copy-start.6 = (f32[128]{0:T(128)S(1)}, f32[128]{0:T(128)}, u32[]{:S(2)}) copy-start(f32[128]{0:T(128)} %param.19) | copy-start | bytes 1540
  4.7 1.2 %copy-start.1 = (bf16[1024,512]{1,0:T(8,128)(2,1)S(1)}, bf16[1024,512]{1,0:T(8,128)(2,1)}, u32[]{:S(2)}) copy-start(bf16[1024,512]{1,0:T(8,128)(2,1)} %w_right_ref.3) | copy-start | bytes 3145732
  5.9 0.9 %copy-start.4 = (bf16[1,64,1024]{2,1,0:T(8,128)(2,1)S(1)}, bf16[1,64,1024]{2,1,0:T(8,128)(2,1)}, u32[]{:S(2)}) copy-start(bf16[1,64,1024]{2,1,0:T(8,128)(2,1)} %param.10) | copy-start | bytes 393220
  6.8 28.0 %copy-start.2 = (bf16[1024,512]{1,0:T(8,128)(2,1)S(1)}, bf16[1024,512]{1,0:T(8,128)(2,1)}, u32[]{:S(2)}) copy-start(bf16[1024,512]{1,0:T(8,128)(2,1)} %w_right_ref.3) | copy-start | bytes 3145732

commit v3 on v2

--- a/solution.py
+++ b/solution.py
@@ -10,6 +10,7 @@
 
 ROWS = 16
 COLS = 48
+BATCH = 4
 MESH = pl.DeviceIdType.MESH
 
 
@@ -17,7 +18,7 @@
     left_ref, right_ref, bias_ref, row_ids_ref, col_ids_ref, target_ref, middle_ref, final_ref,
     left_out, right_out, sums_out,
     left_half, right_half, left_full, right_full, right_acc, row_acc, weight_row, target_row,
-    half_middle, left_acc, final_acc, middle_acc,
+    half_middle, left_acc, final_acc, middle_acc, slope_ref, act_ref, second_ref,
 ):
     panel, hidden = left_ref.shape
     span = 3 * panel
@@ -72,38 +73,62 @@
         row_acc[...] = jnp.zeros_like(row_acc)
 
         def chunk_step(step, carry):
-            cols = pl.ds(pl.multiple_of(start + step * COLS, 8), COLS)
-            pairs = ROWS * COLS
-            half = left_half[rows, :][:, None, :] + right_half[cols, :][None, :, :]
-            plus = left_full[rows, :][:, None, :] + right_full[cols, :][None, :, :]
-            gate = 1.0 + jnp.tanh(half)
-            act = half * gate
-            slope = gate * (plus - act)
-            act_low = act.astype(jnp.bfloat16).reshape(pairs, hidden)
-            upper_half = jnp.dot(act_low, half_middle[...], preferred_element_type=jnp.float32)
-            upper_gate = 1.0 + jnp.tanh(upper_half)
-            upper_act = upper_half * upper_gate
-            upper_slope = upper_gate * (1.0 + 2.0 * upper_half - upper_act)
-            predicted = jnp.sum(upper_act * final_ref[...], axis=1, keepdims=True)
+            first_col = pl.multiple_of(start + step * COLS, 8)
+            cols = pl.ds(first_col, COLS)
             weights = weight_row[tile, cols, :]
-            goal = target_row[tile, cols, :]
-            weights = jnp.concatenate([weights[:, a:a + 1] for a in range(ROWS)], axis=0)
-            goal = jnp.concatenate([goal[:, a:a + 1] for a in range(ROWS)], axis=0)
-            pair_slope = weights * predicted - goal
-            final_acc[...] += jnp.sum(
-                (upper_act * pair_slope).reshape(pairs // 8, 8, upper), axis=0
-            )
-            second = (pair_slope * half_final * upper_slope).astype(jnp.bfloat16)
+            goals = target_row[tile, cols, :]
+
+            def open_part(part):
+                for row in range(part * BATCH, (part + 1) * BATCH):
+                    at = tile * ROWS + row
+                    pairs = slice(row * COLS, (row + 1) * COLS)
+                    half = left_half[at:at + 1, :] + right_half[cols, :]
+                    plus = left_full[at:at + 1, :] + right_full[cols, :]
+                    gate = 1.0 + jnp.tanh(half)
+                    act = half * gate
+                    slope_ref[pairs, :] = gate * (plus - act)
+                    act_ref[pairs, :] = act.astype(jnp.bfloat16)
+
+            def part_pairs(part):
+                return slice(part * BATCH * COLS, (part + 1) * BATCH * COLS)
+
+            open_part(0)
+            for part in range(ROWS // BATCH):
+                pairs = part_pairs(part)
+                upper_half = jnp.dot(
+                    act_ref[pairs, :], half_middle[...], preferred_element_type=jnp.float32
+                )
+                if part + 1 < ROWS // BATCH:
+                    open_part(part + 1)
+                upper_gate = 1.0 + jnp.tanh(upper_half)
+                upper_act = upper_half * upper_gate
+                upper_slope = upper_gate * (1.0 + 2.0 * upper_half - upper_act)
+                predicted = jnp.sum(upper_act * final_ref[...], axis=1, keepdims=True)
+                lanes_of = range(part * BATCH, (part + 1) * BATCH)
+                weight = jnp.concatenate([weights[:, a:a + 1] for a in lanes_of], axis=0)
+                goal = jnp.concatenate([goals[:, a:a + 1] for a in lanes_of], axis=0)
+                pair_slope = weight * predicted - goal
+                final_acc[...] += jnp.sum(
+                    (upper_act * pair_slope).reshape(BATCH * COLS // 8, 8, upper), axis=0
+                )
+                second = (pair_slope * half_final * upper_slope).astype(jnp.bfloat16)
+                second_ref[pairs, :] = second
+                back = lax.dot_general(
+                    second, half_middle[...], (((1,), (1,)), ((), ())),
+                    preferred_element_type=jnp.float32,
+                )
+                across = jnp.zeros((COLS, hidden), jnp.float32)
+                for row in range(BATCH):
+                    index = part * BATCH + row
+                    grad = back[row * COLS:(row + 1) * COLS, :]
+                    grad = grad * slope_ref[index * COLS:(index + 1) * COLS, :]
+                    across = across + grad
+                    row_acc[index] += jnp.sum(grad.reshape(COLS // 8, 8, hidden), axis=0)
+                right_acc[cols, :] += across
             middle_acc[...] += lax.dot_general(
-                second, act_low, (((0,), (0,)), ((), ())), preferred_element_type=jnp.float32
-            )
-            back = lax.dot_general(
-                second, half_middle[...], (((1,), (1,)), ((), ())),
+                second_ref[...], act_ref[...], (((0,), (0,)), ((), ())),
                 preferred_element_type=jnp.float32,
             )
-            grad = back.reshape(ROWS, COLS, hidden) * slope
-            row_acc[...] += jnp.sum(grad.reshape(ROWS, COLS // 8, 8, hidden), axis=1)
-            right_acc[cols, :] += jnp.sum(grad, axis=0)
             return carry
 
         lax.fori_loop(0, chunks, chunk_step, 0)
@@ -146,6 +171,9 @@
             pltpu.VMEM((panel, hidden), f32),
             pltpu.VMEM((8, upper), f32),
             pltpu.VMEM((upper, hidden), f32),
+            pltpu.VMEM((ROWS * COLS, hidden), f32),
+            pltpu.VMEM((ROWS * COLS, hidden), jnp.bfloat16),
+            pltpu.VMEM((ROWS * COLS, upper), jnp.bfloat16),
         ],
         compiler_params=pltpu.CompilerParams(vmem_limit_bytes=32 * 1024 * 1024),
         name="pair_grads",
@@ -307,10 +335,10 @@
     mine_g[...] = right.astype(bf16)
     share(1)
     forward(0)
-    emb_out[...] = lax.dot_general(
-        left_ref[...], w_left_ref[...], (((1,), (1,)), ((), ())), preferred_element_type=f32
-    )
     multiply(0)
+    forward(1)
+    multiply(1)
+    combine(0)
     small_sum = small[blk].astype(f32)
     for step in range(1, n_blk):
         slot = small_in.at[step]
@@ -323,30 +351,7 @@
         copy(slot, slot, sz_send.at[step], sz_recv.at[step], lax.rem(grp + step, n_grp), blk).start()
         return carry
     lax.fori_loop(1, n_grp, small_across, 0)
-    forward(1)
-    emb_out[...] += lax.dot_general(
-        mine_g[...], w_right_ref[...], (((1,), (1,)), ((), ())), preferred_element_type=f32
-    )
-    multiply(1)
-    combine(0)
-
-    def small_take(step, carry):
-        slot = small_z.at[lax.rem(grp + n_grp - step, n_grp)]
-        copy(slot, slot, sz_send.at[step], sz_recv.at[step], grp, blk).wait_recv()
-        return carry
-    lax.fori_loop(1, n_grp, small_take, 0)
-    small_total = small_z[0].astype(f32)
-    for group in range(1, n_grp):
-        small_total = small_total + small_z[group].astype(f32)
-    small_out[blk] = small_total.astype(bf16)
-
-    def small_spread(step, carry):
-        slot = small_out.at[blk]
-        copy(
-            slot, slot, sa_send.at[step], sa_recv.at[step], grp, lax.rem(blk + step, n_blk)
-        ).start()
-        return carry
-    lax.fori_loop(1, n_blk, small_spread, 0)
+
     combine(1)
     for half in range(2):
         def pass_on(step, carry):
@@ -357,6 +362,23 @@
             return carry
         lax.fori_loop(1, n_grp, pass_on, 0)
 
+    def small_take(step, carry):
+        slot = small_z.at[lax.rem(grp + n_grp - step, n_grp)]
+        copy(slot, slot, sz_send.at[step], sz_recv.at[step], grp, blk).wait_recv()
+        return carry
+    lax.fori_loop(1, n_grp, small_take, 0)
+    small_total = small_z[0].astype(f32)
+    for group in range(1, n_grp):
+        small_total = small_total + small_z[group].astype(f32)
+    small_out[blk] = small_total.astype(bf16)
+
+    def small_spread(step, carry):
+        slot = small_out.at[blk]
+        copy(
+            slot, slot, sa_send.at[step], sa_recv.at[step], grp, lax.rem(blk + step, n_blk)
+        ).start()
+        return carry
+    lax.fori_loop(1, n_blk, small_spread, 0)
     def hand_on(index, carry):
         half, rest = index // n_grp, lax.rem(index, n_grp)
         part = lax.rem(grp + n_grp - rest, n_grp)
@@ -371,6 +393,12 @@
             ).start()
             return inner
         return lax.fori_loop(1, chips, hand, carry)
+    emb_out[...] = lax.dot_general(
+        left_ref[...], w_left_ref[...], (((1,), (1,)), ((), ())), preferred_element_type=f32
+    )
+    emb_out[...] += lax.dot_general(
+        mine_g[...], w_right_ref[...], (((1,), (1,)), ((), ())), preferred_element_type=f32
+    )
     lax.fori_loop(0, 2 * n_grp, hand_on, 0)
 
     def finish(index, carry):
@@ -568,24 +596,30 @@
     ids_mine[...] = jnp.broadcast_to(ids_ref[...], ids_mine.shape)
     ids_out[1] = ids_mine[...]
 
-    def sum_pair(index, carry):
-        to, offset = index // 3, lax.rem(index, 3)
-        total = jnp.zeros((fold, lanes), f32)
-        number = jnp.zeros((8, lanes), f32)
-        for slot in range(slots):
-            row, col = block_ref[slot, 0], block_ref[slot, 1]
-            hit = (row == to) & (col - row == offset - 1) & (slot < count_ref[0, 0])
-            weight = jnp.where(hit, 1.0, 0.0).astype(f32)
-            total = total + weight * target_ref[slot]
-            number = number + weight
-        target_mine[to, offset, 0:fold, :] = total
-        target_mine[to, offset, fold:fold + 8, :] = number
-        return carry
-    lax.fori_loop(0, 3 * n_blk, sum_pair, 0)
     pl.semaphore_wait(barrier, n_blk - 1)
+
+    def send_emb(step, carry):
+        to = lax.rem(blk + step, n_blk)
+        copy(emb_cols.at[to], emb_out.at[blk], e_send.at[step], e_recv.at[step], to).start()
+        return carry
+    lax.fori_loop(1, n_blk, send_emb, 0)
+
+    def sum_pairs(to):
+        for offset in range(3):
+            total = jnp.zeros((fold, lanes), f32)
+            number = jnp.zeros((8, lanes), f32)
+            for slot in range(slots):
+                row, col = block_ref[slot, 0], block_ref[slot, 1]
+                hit = (row == to) & (col - row == offset - 1) & (slot < count_ref[0, 0])
+                weight = jnp.where(hit, 1.0, 0.0).astype(f32)
+                total = total + weight * target_ref[slot]
+                number = number + weight
+            target_mine[to, offset, 0:fold, :] = total
+            target_mine[to, offset, fold:fold + 8, :] = number
 
     def send_targets(step, carry):
         to = lax.rem(blk + step, n_blk)
+        sum_pairs(to)
         copy(target_mine.at[to], target_in.at[step], t_send.at[step], t_recv.at[step], to).start()
         return carry
     lax.fori_loop(1, n_blk, send_targets, 0)
@@ -602,15 +636,10 @@
     for exchange in exchanges:
         exchange.start()
 
-    def send_emb(step, carry):
-        to = lax.rem(blk + step, n_blk)
-        copy(emb_cols.at[to], emb_out.at[blk], e_send.at[step], e_recv.at[step], to).start()
-        return carry
-    lax.fori_loop(1, n_blk, send_emb, 0)
-
     fetch_left.wait()
     left_out[...] = jnp.dot(emb_ref[...], w_both[0], preferred_element_type=f32).astype(bf16)
     emb_out[blk] = emb_cols[blk]
+    sum_pairs(blk)
     target_out[...] = target_mine[blk]
 
     def take_targets(step, carry):
@@ -661,7 +690,7 @@
             dma((2,)), dma((2,)), dma((2,)), dma((2,)),
         ],
         compiler_params=pltpu.CompilerParams(
-            collective_id=2, has_side_effects=True, vmem_limit_bytes=32 * 1024 * 1024
+            collective_id=2, has_side_effects=True, vmem_limit_bytes=56 * 1024 * 1024
         ),
         name="gather_panels",
     )(emb, w_left, w_right, ids, targets, blocks, counts)

time: 86.1 us -> 94.8 us (1.10); the launches traced: 85 us -> 95.8 us
  Pallas kernels: 77.4 us -> 84.1 us
  local copies, waits for them, and re-layouts: 5.48 us -> 9.6 us
    pallas_call x1, Pallas kernels: 46.6 us -> 53.7 us  [reduce_grads(): pl.pallas_call(functools.partial(reduce_kernel, n_grp, n_blk, scale), out...]
    unnamed x15 -> x21, local copies, waits for them, and re-layouts: 2.85 us -> 5.1 us
    pallas_call x1, Pallas kernels: 12.7 us -> 11.7 us  [pair_grads(): pl.pallas_call(pair_kernel, out_shape=(jax.ShapeDtypeStruct((panel, hidde...]
where the time goes in v3:
time: 94.8 us; the launch traced here: 95.8 us
  Pallas kernels  84.1 us (89%)
  local copies, waits for them, and re-layouts  9.6 us (10%)
  between operations  1.39 us (1%)
    pallas_call x1, Pallas kernels, reduce_grads(): pl.pallas_call(functools.partial(reduce_kernel, n_grp, n_blk, scale), out...  53.7 us
    pallas_call x1, Pallas kernels, gather_panels(): pl.pallas_call(functools.partial(gather_kernel, n_blk), out_shape=(jax.Sh...  15.9 us
    pallas_call x1, Pallas kernels, pair_grads(): pl.pallas_call(pair_kernel, out_shape=(jax.ShapeDtypeStruct((panel, hidde...  11.7 us
    unnamed x21, local copies, waits for them, and re-layouts  5.1 us
    pallas_call x1, Pallas kernels, unpack_grads(): pl.pallas_call(functools.partial(unpack_kernel, scale), grid=(steps,), ou...  2.85 us

profile of v3, /device:TPU:0, one launch (start us, length us, event | category | flops | bytes accessed | tf_op | source)
XLA Modules:
  0.0 95.8 jit_solution(8169482204425783636)
XLA Ops:
  1.3 0.7 fusion
  1.9 1.3 %copy.21.block_ref = s32[8,2]{1,0:T(8,128)} copy(s32[8,2]{0,1:T(2,128)} %bitcast.15) | data formatting | bytes 128 | tf_op jit(solution)/shard_map/squeeze | solution.py:716
  3.3 0.7 copy.20.ids_ref
  4.0 1.4 %reshape_squeeze.3 = f32[8,64,2,32]{3,2,1,0:T(2,128)S(1)} reshape(f32[1,8,4096]{2,1,0:T(8,128)} %param.14) | data formatting | bytes 262144 | tf_op jit(solution)/shard_map/reshape;squeeze | solution.py:712
  5.4 0.0 copy-start
  5.4 0.0 copy-start.1
  5.4 0.2 copy.19
  5.6 0.8 reshape.26.target_ref
  6.5 15.9 %gather_panels.1 = (bf16[64,512]{1,0:T(8,128)(2,1)}, bf16[3,64,512]{2,1,0:T(8,128)(2,1)}, f32[3,64,128]{2,1,0:T(8,128)}, f32[3,40,128]{2,1,0:T(8,128)}, bf16[8,64,128]{2,1,0:T(8,128)(2,1)}) custom-call(bf16[64,1024]{1,0:T(8,128)(2,1)} %bitcast.14, bf16[1024,512]{1,0:T(8,128)(2,1)} %w_left_ref.3, bf16[1024,512]{1,0:T(8,128)(2,1)} %w_right_ref.3, ...), custom_call_target="tpu_custom_call" | custom-call | tf_op jit(solution)/shard_map/gather_panels/pallas_call | solution.py:671
  22.4 0.0 copy-done.4
  22.4 0.0 copy-done.8
  22.4 0.0 copy-done.9
  22.4 0.0 copy-start.2
  22.5 0.9 copy-done.2
  23.4 0.9 copy-done.5
  24.3 0.8 copy-done.6
  25.1 0.8 copy-done.7
  25.9 11.7 %pair_grads.1 = (bf16[64,512]{1,0:T(8,128)(2,1)S(1)}, bf16[3,64,512]{2,1,0:T(8,128)(2,1)S(1)}, bf16[144,512]{1,0:T(8,128)(2,1)S(1)}) custom-call(bf16[64,512]{1,0:T(8,128)(2,1)S(1)} %copy-done.6, bf16[3,64,512]{2,1,0:T(8,128)(2,1)S(1)} %copy-done.2, f32[1,512]{1,0:T(1,128)S(1)} %bitcast.11, f32[1,64]{1,0:T(1,128)S(1)} %get-tuple-element.38.row_ids_ref, ...), custom_call_target="tpu_custom_call" | custom-call | tf_op jit(solution)/shard_map/pair_grads/pallas_call | solution.py:152
  37.6 0.0 copy-done
  37.6 0.0 copy-done.1
  37.6 0.9 copy-done.3
  38.5 53.7 %reduce_grads.1 = (f32[64,1024]{1,0:T(8,128)S(1)}, bf16[2,8,4,128,128]{4,3,2,1,0:T(8,128)(2,1)S(1)}, bf16[8,5,16,128]{3,2,1,0:T(8,128)(2,1)S(1)}) custom-call(bf16[64,512]{1,0:T(8,128)(2,1)S(1)} %get-tuple-element.26.left_ref, bf16[3,64,512]{2,1,0:T(8,128)(2,1)S(1)} %get-tuple-element.27.right_ref, bf16[8,64,128]{2,1,0:T(8,128)(2,1)S(1)} %copy-done.3, ...), custom_call_target="tpu_custom_call" | custom-call | tf_op jit(solution)/shard_map/reduce_grads/pallas_call | solution.py:470
  92.2 2.8 %unpack_grads.1 = (f32[1024,512]{1,0:T(8,128)}, f32[1024,512]{1,0:T(8,128)}, f32[1,512]{1,0:T(1,128)}, f32[512,128]{1,0:T(8,128)}, f32[1,128]{1,0:T(1,128)}) custom-call(bf16[2,8,4,128,128]{4,3,2,1,0:T(8,128)(2,1)S(1)} %get-tuple-element.31.pieces_ref, bf16[8,5,16,128]{3,2,1,0:T(8,128)(2,1)S(1)} %get-tuple-element.32.small_ref), custom_call_target="tpu_custom_call" | custom-call | tf_op jit(solution)/shard_map/unpack_grads/pallas_call | solution.py:536
  95.1 0.7 copy.24
  (7 shorter events, 0.0 us)
Async XLA Ops:
  4.0 18.4 %copy-start.4 = (bf16[512,128]{1,0:T(8,128)(2,1)S(1)}, bf16[512,128]{1,0:T(8,128)(2,1)}, u32[]{:S(2)}) copy-start(bf16[512,128]{1,0:T(8,128)(2,1)} %middle_ref.1) | copy-start | bytes 393220
  4.0 18.4 %copy-start.8 = (f32[512]{0:T(512)S(1)}, f32[512]{0:T(512)}, u32[]{:S(2)}) copy-start(f32[512]{0:T(512)} %param.17) | copy-start | bytes 6148
  4.0 18.4 %copy-start.9 = (f32[128]{0:T(128)S(1)}, f32[128]{0:T(128)}, u32[]{:S(2)}) copy-start(f32[128]{0:T(128)} %param.19) | copy-start | bytes 1540
  5.4 32.2 %copy-start = (bf16[1024,512]{1,0:T(8,128)(2,1)S(1)}, bf16[1024,512]{1,0:T(8,128)(2,1)}, u32[]{:S(2)}) copy-start(bf16[1024,512]{1,0:T(8,128)(2,1)} %w_left_ref.3) | copy-start | bytes 3145732
  5.4 32.2 %copy-start.1 = (bf16[1024,512]{1,0:T(8,128)(2,1)S(1)}, bf16[1024,512]{1,0:T(8,128)(2,1)}, u32[]{:S(2)}) copy-start(bf16[1024,512]{1,0:T(8,128)(2,1)} %w_right_ref.3) | copy-start | bytes 3145732
  22.4 0.9 copy-start.2
  23.4 0.9 copy-start.5
  24.3 0.8 copy-start.6
  25.1 0.8 copy-start.7
  37.6 0.9 copy-start.3

commit v4 on v3

--- a/solution.py
+++ b/solution.py
@@ -17,8 +17,9 @@
 def pair_kernel(
     left_ref, right_ref, bias_ref, row_ids_ref, col_ids_ref, target_ref, middle_ref, final_ref,
     left_out, right_out, sums_out,
-    left_half, right_half, left_full, right_full, right_acc, row_acc, weight_row, target_row,
+    left_half, right_half, right_acc, row_acc, weight_row, target_row,
     half_middle, left_acc, final_acc, middle_acc, slope_ref, act_ref, second_ref,
+    half_middle_t,
 ):
     panel, hidden = left_ref.shape
     span = 3 * panel
@@ -26,14 +27,12 @@
     upper = middle_ref.shape[1]
     fold = target_ref.shape[1] - 8
     half_middle[...] = middle_ref[...] * jnp.bfloat16(0.5)
+    half_middle_t[...] = half_middle[...].T
     left = left_ref[...].astype(jnp.float32)
     right = right_ref[...].astype(jnp.float32).reshape(span, hidden) + bias_ref[...]
     left_half[...] = 0.5 * left
     right_half[0:span, :] = 0.5 * right
     right_half[span:padded, :] = jnp.zeros((padded - span, hidden), jnp.float32)
-    left_full[...] = left
-    right_full[0:span, :] = right + 1.0
-    right_full[span:padded, :] = jnp.zeros((padded - span, hidden), jnp.float32)
     right_acc[...] = jnp.zeros_like(right_acc)
     middle_acc[...] = jnp.zeros_like(middle_acc)
     final_acc[...] = jnp.zeros_like(final_acc)
@@ -82,12 +81,11 @@
                 for row in range(part * BATCH, (part + 1) * BATCH):
                     at = tile * ROWS + row
                     pairs = slice(row * COLS, (row + 1) * COLS)
-                    half = left_half[at:at + 1, :] + right_half[cols, :]
-                    plus = left_full[at:at + 1, :] + right_full[cols, :]
+                    half = (left_half[at:at + 1, :] + right_half[cols, :]).astype(jnp.bfloat16)
                     gate = 1.0 + jnp.tanh(half)
                     act = half * gate
-                    slope_ref[pairs, :] = gate * (plus - act)
-                    act_ref[pairs, :] = act.astype(jnp.bfloat16)
+                    slope_ref[pairs, :] = gate * ((half + half) + (1.0 - act))
+                    act_ref[pairs, :] = act
 
             def part_pairs(part):
                 return slice(part * BATCH * COLS, (part + 1) * BATCH * COLS)
@@ -113,15 +111,12 @@
                 )
                 second = (pair_slope * half_final * upper_slope).astype(jnp.bfloat16)
                 second_ref[pairs, :] = second
-                back = lax.dot_general(
-                    second, half_middle[...], (((1,), (1,)), ((), ())),
-                    preferred_element_type=jnp.float32,
-                )
+                back = jnp.dot(second, half_middle_t[...], preferred_element_type=jnp.float32)
                 across = jnp.zeros((COLS, hidden), jnp.float32)
                 for row in range(BATCH):
                     index = part * BATCH + row
                     grad = back[row * COLS:(row + 1) * COLS, :]
-                    grad = grad * slope_ref[index * COLS:(index + 1) * COLS, :]
+                    grad = grad * slope_ref[index * COLS:(index + 1) * COLS, :].astype(jnp.float32)
                     across = across + grad
                     row_acc[index] += jnp.sum(grad.reshape(COLS // 8, 8, hidden), axis=0)
                 right_acc[cols, :] += across
@@ -161,8 +156,6 @@
         scratch_shapes=[
             pltpu.VMEM((panel, hidden), f32),
             pltpu.VMEM((padded, hidden), f32),
-            pltpu.VMEM((panel, hidden), f32),
-            pltpu.VMEM((padded, hidden), f32),
             pltpu.VMEM((padded, hidden), f32),
             pltpu.VMEM((ROWS, 8, hidden), f32),
             pltpu.VMEM((panel // ROWS, padded, ROWS), f32),
@@ -171,9 +164,10 @@
             pltpu.VMEM((panel, hidden), f32),
             pltpu.VMEM((8, upper), f32),
             pltpu.VMEM((upper, hidden), f32),
-            pltpu.VMEM((ROWS * COLS, hidden), f32),
+            pltpu.VMEM((ROWS * COLS, hidden), jnp.bfloat16),
             pltpu.VMEM((ROWS * COLS, hidden), jnp.bfloat16),
             pltpu.VMEM((ROWS * COLS, upper), jnp.bfloat16),
+            pltpu.VMEM((upper, hidden), jnp.bfloat16),
         ],
         compiler_params=pltpu.CompilerParams(vmem_limit_bytes=32 * 1024 * 1024),
         name="pair_grads",
@@ -690,7 +684,7 @@
             dma((2,)), dma((2,)), dma((2,)), dma((2,)),
         ],
         compiler_params=pltpu.CompilerParams(
-            collective_id=2, has_side_effects=True, vmem_limit_bytes=56 * 1024 * 1024
+            collective_id=2, has_side_effects=True, vmem_limit_bytes=32 * 1024 * 1024
         ),
         name="gather_panels",
     )(emb, w_left, w_right, ids, targets, blocks, counts)

time: 94.8 us -> 87.2 us (0.920); the launches traced: 95.8 us -> 86.1 us
  Pallas kernels: 84.1 us -> 78.5 us
  local copies, waits for them, and re-layouts: 9.6 us -> 5.48 us
    pallas_call x1, Pallas kernels: 53.7 us -> 39.1 us  [reduce_grads(): pl.pallas_call(functools.partial(reduce_kernel, n_grp, n_blk, scale), out...]
    pallas_call x1, Pallas kernels: 11.7 us -> 21.6 us  [pair_grads(): pl.pallas_call(pair_kernel, out_shape=(jax.ShapeDtypeStruct((panel, hidde...]
    unnamed x21 -> x15, local copies, waits for them, and re-layouts: 5.1 us -> 2.85 us
    pallas_call x1, Pallas kernels: 15.9 us -> 14.9 us  [gather_panels(): pl.pallas_call(functools.partial(gather_kernel, n_blk), out_shape=(jax.Sh...]
where the time goes in v4:
time: 87.2 us; the launch traced here: 86.1 us
  Pallas kernels  78.5 us (90%)
  local copies, waits for them, and re-layouts  5.48 us (6%)
  between operations  1.47 us (2%)
    pallas_call x1, Pallas kernels, reduce_grads(): pl.pallas_call(functools.partial(reduce_kernel, n_grp, n_blk, scale), out...  39.1 us
    pallas_call x1, Pallas kernels, pair_grads(): pl.pallas_call(pair_kernel, out_shape=(jax.ShapeDtypeStruct((panel, hidde...  21.6 us
    pallas_call x1, Pallas kernels, gather_panels(): pl.pallas_call(functools.partial(gather_kernel, n_blk), out_shape=(jax.Sh...  14.9 us
    unnamed x15, local copies, waits for them, and re-layouts  2.85 us
    pallas_call x1, Pallas kernels, unpack_grads(): pl.pallas_call(functools.partial(unpack_kernel, scale), grid=(steps,), ou...  2.85 us

profile of v4, /device:TPU:0, one launch (start us, length us, event | category | flops | bytes accessed | tf_op | source)
XLA Modules:
  0.0 86.1 jit_solution(2890281488829720449)
XLA Ops:
  0.6 0.0 copy-start
  1.4 0.7 fusion
  2.0 0.8 copy.21.block_ref
  2.8 0.1 copy.20.ids_ref
  2.9 0.0 copy-start.3
  2.9 0.0 copy-start.5
  2.9 0.0 copy-start.6
  2.9 1.4 %reshape_squeeze.3 = f32[8,64,2,32]{3,2,1,0:T(2,128)S(1)} reshape(f32[1,8,4096]{2,1,0:T(8,128)} %param.14) | data formatting | bytes 262144 | tf_op jit(solution)/shard_map/reshape;squeeze | solution.py:706
  4.3 0.2 copy.19
  4.5 0.2 reshape.26.target_ref
  4.7 0.0 copy-done
  4.7 1.2 %copy-done.1 = bf16[1024,512]{1,0:T(8,128)(2,1)S(1)} copy-done((bf16[1024,512]{1,0:T(8,128)(2,1)S(1)}, bf16[1024,512]{1,0:T(8,128)(2,1)}, u32[]{:S(2)}) %copy-start.1) | copy-done | bytes 1048600
  5.9 0.0 copy-start.4
  5.9 0.9 %copy-done.4 = bf16[1,64,1024]{2,1,0:T(8,128)(2,1)S(1)} copy-done((bf16[1,64,1024]{2,1,0:T(8,128)(2,1)S(1)}, bf16[1,64,1024]{2,1,0:T(8,128)(2,1)}, u32[]{:S(2)}) %copy-start.4) | copy-done | bytes 131096
  6.8 0.0 copy-start.2
  6.8 14.9 %gather_panels.1 = (bf16[64,512]{1,0:T(8,128)(2,1)S(1)}, bf16[3,64,512]{2,1,0:T(8,128)(2,1)S(1)}, f32[3,64,128]{2,1,0:T(8,128)S(1)}, f32[3,40,128]{2,1,0:T(8,128)S(1)}, bf16[8,64,128]{2,1,0:T(8,128)(2,1)S(1)}) custom-call(bf16[64,1024]{1,0:T(8,128)(2,1)S(1)} %bitcast.11, bf16[1024,512]{1,0:T(8,128)(2,1)S(1)} %copy-done, bf16[1024,512]{1,0:T(8,128)(2,1)S(1)} %copy-done.1, ...), custom_call_target="tpu_custom_call" | custom-call | tf_op jit(solution)/shard_map/gather_panels/pallas_call | solution.py:665
  21.7 0.0 copy-done.3
  21.7 0.0 copy-done.5
  21.7 0.0 copy-done.6
  21.7 21.6 %pair_grads.1 = (bf16[64,512]{1,0:T(8,128)(2,1)S(1)}, bf16[3,64,512]{2,1,0:T(8,128)(2,1)S(1)}, bf16[144,512]{1,0:T(8,128)(2,1)S(1)}) custom-call(bf16[64,512]{1,0:T(8,128)(2,1)S(1)} %get-tuple-element.22.left_ref, bf16[3,64,512]{2,1,0:T(8,128)(2,1)S(1)} %get-tuple-element.23.right_ref, f32[1,512]{1,0:T(1,128)S(1)} %bitcast.12, ...), custom_call_target="tpu_custom_call" | custom-call | tf_op jit(solution)/shard_map/pair_grads/pallas_call | solution.py:147
  43.4 0.0 copy-done.2
  43.4 39.1 %reduce_grads.1 = (f32[64,1024]{1,0:T(8,128)S(1)}, bf16[2,8,4,128,128]{4,3,2,1,0:T(8,128)(2,1)S(1)}, bf16[8,5,16,128]{3,2,1,0:T(8,128)(2,1)S(1)}) custom-call(bf16[64,512]{1,0:T(8,128)(2,1)S(1)} %get-tuple-element.26.left_ref, bf16[3,64,512]{2,1,0:T(8,128)(2,1)S(1)} %get-tuple-element.27.right_ref, bf16[8,64,128]{2,1,0:T(8,128)(2,1)S(1)} %get-tuple-element.28.emb_ref, ...), custom_call_target="tpu_custom_call" | custom-call | tf_op jit(solution)/shard_map/reduce_grads/pallas_call | solution.py:464
  82.5 2.8 %unpack_grads.1 = (f32[1024,512]{1,0:T(8,128)}, f32[1024,512]{1,0:T(8,128)}, f32[1,512]{1,0:T(1,128)}, f32[512,128]{1,0:T(8,128)}, f32[1,128]{1,0:T(1,128)}) custom-call(bf16[2,8,4,128,128]{4,3,2,1,0:T(8,128)(2,1)S(1)} %get-tuple-element.31.pieces_ref, bf16[8,5,16,128]{3,2,1,0:T(8,128)(2,1)S(1)} %get-tuple-element.32.small_ref), custom_call_target="tpu_custom_call" | custom-call | tf_op jit(solution)/shard_map/unpack_grads/pallas_call | solution.py:530
  85.4 0.7 copy.24
  (1 shorter events, 0.0 us)
Async XLA Ops:
  0.6 4.1 %copy-start = (bf16[1024,512]{1,0:T(8,128)(2,1)S(1)}, bf16[1024,512]{1,0:T(8,128)(2,1)}, u32[]{:S(2)}) copy-start(bf16[1024,512]{1,0:T(8,128)(2,1)} %w_left_ref.3) | copy-start | bytes 3145732
  2.9 18.8 %copy-start.3 = (bf16[512,128]{1,0:T(8,128)(2,1)S(1)}, bf16[512,128]{1,0:T(8,128)(2,1)}, u32[]{:S(2)}) copy-start(bf16[512,128]{1,0:T(8,128)(2,1)} %middle_ref.1) | copy-start | bytes 393220
  2.9 18.8 %copy-start.5 = (f32[512]{0:T(512)S(1)}, f32[512]{0:T(512)}, u32[]{:S(2)}) copy-start(f32[512]{0:T(512)} %param.17) | copy-start | bytes 6148
  2.9 18.8 %copy-start.6 = (f32[128]{0:T(128)S(1)}, f32[128]{0:T(128)}, u32[]{:S(2)}) copy-start(f32[128]{0:T(128)} %param.19) | copy-start | bytes 1540
  4.7 1.2 %copy-start.1 = (bf16[1024,512]{1,0:T(8,128)(2,1)S(1)}, bf16[1024,512]{1,0:T(8,128)(2,1)}, u32[]{:S(2)}) copy-start(bf16[1024,512]{1,0:T(8,128)(2,1)} %w_right_ref.3) | copy-start | bytes 3145732
  5.9 0.9 %copy-start.4 = (bf16[1,64,1024]{2,1,0:T(8,128)(2,1)S(1)}, bf16[1,64,1024]{2,1,0:T(8,128)(2,1)}, u32[]{:S(2)}) copy-start(bf16[1,64,1024]{2,1,0:T(8,128)(2,1)} %param.10) | copy-start | bytes 393220
  6.8 36.5 %copy-start.2 = (bf16[1024,512]{1,0:T(8,128)(2,1)S(1)}, bf16[1024,512]{1,0:T(8,128)(2,1)}, u32[]{:S(2)}) copy-start(bf16[1024,512]{1,0:T(8,128)(2,1)} %w_right_ref.3) | copy-start | bytes 3145732

commit v5 on v4

--- a/solution.py
+++ b/solution.py
@@ -17,7 +17,7 @@
 def pair_kernel(
     left_ref, right_ref, bias_ref, row_ids_ref, col_ids_ref, target_ref, middle_ref, final_ref,
     left_out, right_out, sums_out,
-    left_half, right_half, right_acc, row_acc, weight_row, target_row,
+    left_half, right_half, right_acc, row_acc, coded, spread, ones,
     half_middle, left_acc, final_acc, middle_acc, slope_ref, act_ref, second_ref,
     half_middle_t,
 ):
@@ -52,10 +52,18 @@
     tiles = panel // ROWS
     active = jnp.where(counts > 0.0, 1.0, 0.0)
     for tile in range(tiles):
-        weight_row[tile, 0:span, :] = counts[:, tile * ROWS:(tile + 1) * ROWS]
-        weight_row[tile, span:padded, :] = jnp.zeros((padded - span, ROWS), jnp.float32)
-        target_row[tile, 0:span, :] = targets[:, tile * ROWS:(tile + 1) * ROWS]
-        target_row[tile, span:padded, :] = jnp.zeros((padded - span, ROWS), jnp.float32)
+        lanes = slice(tile * ROWS, (tile + 1) * ROWS)
+        goal = targets[:, lanes]
+        goal_high = goal.astype(jnp.bfloat16).astype(jnp.float32)
+        coded[tile, 0:span, :] = jnp.concatenate(
+            [counts[:, lanes], goal_high, goal - goal_high,
+             jnp.zeros((span, 128 - 3 * ROWS), jnp.float32)], axis=1
+        )
+        coded[tile, span:padded, :] = jnp.zeros((padded - span, 128), jnp.float32)
+    spread_row = lax.broadcasted_iota(jnp.int32, (128, 2 * upper), 0)
+    spread_col = lax.broadcasted_iota(jnp.int32, (128, 2 * upper), 1)
+    spread[...] = jnp.where((spread_row < ROWS) == (spread_col < upper), 1.0, 0.0).astype(jnp.bfloat16)
+    ones[...] = jnp.ones(ones.shape, jnp.bfloat16)
 
     where_col = (col_pos + panel).astype(jnp.float32)
     first_map = jnp.where(active > 0.0, where_col, float(padded))
@@ -74,8 +82,8 @@
         def chunk_step(step, carry):
             first_col = pl.multiple_of(start + step * COLS, 8)
             cols = pl.ds(first_col, COLS)
-            weights = weight_row[tile, cols, :]
-            goals = target_row[tile, cols, :]
+            code = coded[tile, cols, :]
+            code_row = lax.broadcasted_iota(jnp.int32, (COLS, 128), 1) % ROWS
 
             def open_part(part):
                 for row in range(part * BATCH, (part + 1) * BATCH):
@@ -101,11 +109,19 @@
                 upper_gate = 1.0 + jnp.tanh(upper_half)
                 upper_act = upper_half * upper_gate
                 upper_slope = upper_gate * (1.0 + 2.0 * upper_half - upper_act)
-                predicted = jnp.sum(upper_act * final_ref[...], axis=1, keepdims=True)
-                lanes_of = range(part * BATCH, (part + 1) * BATCH)
-                weight = jnp.concatenate([weights[:, a:a + 1] for a in lanes_of], axis=0)
-                goal = jnp.concatenate([goals[:, a:a + 1] for a in lanes_of], axis=0)
-                pair_slope = weight * predicted - goal
+                terms = upper_act * final_ref[...]
+                terms_high = terms.astype(jnp.bfloat16)
+                terms_low = (terms - terms_high.astype(jnp.float32)).astype(jnp.bfloat16)
+                predicted = jnp.dot(
+                    jnp.concatenate([terms_high, terms_low], axis=1), ones[...],
+                    preferred_element_type=jnp.float32,
+                )
+                picked = jnp.concatenate(
+                    [jnp.where(code_row == a, code, 0.0).astype(jnp.bfloat16)
+                     for a in range(part * BATCH, (part + 1) * BATCH)], axis=0
+                )
+                both = jnp.dot(picked, spread[...], preferred_element_type=jnp.float32)
+                pair_slope = both[:, 0:upper] * predicted - both[:, upper:2 * upper]
                 final_acc[...] += jnp.sum(
                     (upper_act * pair_slope).reshape(BATCH * COLS // 8, 8, upper), axis=0
                 )
@@ -158,8 +174,9 @@
             pltpu.VMEM((padded, hidden), f32),
             pltpu.VMEM((padded, hidden), f32),
             pltpu.VMEM((ROWS, 8, hidden), f32),
-            pltpu.VMEM((panel // ROWS, padded, ROWS), f32),
-            pltpu.VMEM((panel // ROWS, padded, ROWS), f32),
+            pltpu.VMEM((panel // ROWS, padded, 128), f32),
+            pltpu.VMEM((128, 2 * upper), jnp.bfloat16),
+            pltpu.VMEM((2 * upper, upper), jnp.bfloat16),
             pltpu.VMEM((hidden, upper), jnp.bfloat16),
             pltpu.VMEM((panel, hidden), f32),
             pltpu.VMEM((8, upper), f32),

time: 87.2 us -> 82.6 us (0.947); the launches traced: 86.1 us -> 82.5 us
  Pallas kernels: 78.5 us -> 74.9 us
    pallas_call x1, Pallas kernels: 21.6 us -> 9.21 us  [pair_grads(): pl.pallas_call(pair_kernel, out_shape=(jax.ShapeDtypeStruct((panel, hidde...]
    pallas_call x1, Pallas kernels: 39.1 us -> 47.9 us  [reduce_grads(): pl.pallas_call(functools.partial(reduce_kernel, n_grp, n_blk, scale), out...]
where the time goes in v5:
time: 82.6 us; the launch traced here: 82.5 us
  Pallas kernels  74.9 us (91%)
  local copies, waits for them, and re-layouts  5.48 us (7%)
  between operations  1.47 us (2%)
    pallas_call x1, Pallas kernels, reduce_grads(): pl.pallas_call(functools.partial(reduce_kernel, n_grp, n_blk, scale), out...  47.9 us
    pallas_call x1, Pallas kernels, gather_panels(): pl.pallas_call(functools.partial(gather_kernel, n_blk), out_shape=(jax.Sh...  14.9 us
    pallas_call x1, Pallas kernels, pair_grads(): pl.pallas_call(pair_kernel, out_shape=(jax.ShapeDtypeStruct((panel, hidde...  9.21 us
    unnamed x15, local copies, waits for them, and re-layouts  2.85 us
    pallas_call x1, Pallas kernels, unpack_grads(): pl.pallas_call(functools.partial(unpack_kernel, scale), grid=(steps,), ou...  2.85 us

profile of v5, /device:TPU:0, one launch (start us, length us, event | category | flops | bytes accessed | tf_op | source)
XLA Modules:
  0.0 82.5 jit_solution(16908160562351617410)
XLA Ops:
  0.6 0.0 copy-start
  1.4 0.7 fusion
  2.0 0.8 copy.21.block_ref
  2.8 0.1 copy.20.ids_ref
  2.9 0.0 copy-start.3
  2.9 0.0 copy-start.5
  2.9 0.0 copy-start.6
  2.9 1.4 %reshape_squeeze.3 = f32[8,64,2,32]{3,2,1,0:T(2,128)S(1)} reshape(f32[1,8,4096]{2,1,0:T(8,128)} %param.14) | data formatting | bytes 262144 | tf_op jit(solution)/shard_map/reshape;squeeze | solution.py:723
  4.3 0.2 copy.19
  4.5 0.2 reshape.26.target_ref
  4.7 0.0 copy-done
  4.7 0.0 copy-start.1
  4.7 1.2 %copy-done.1 = bf16[1024,512]{1,0:T(8,128)(2,1)S(1)} copy-done((bf16[1024,512]{1,0:T(8,128)(2,1)S(1)}, bf16[1024,512]{1,0:T(8,128)(2,1)}, u32[]{:S(2)}) %copy-start.1) | copy-done | bytes 1048600
  5.9 0.0 copy-start.4
  5.9 0.9 %copy-done.4 = bf16[1,64,1024]{2,1,0:T(8,128)(2,1)S(1)} copy-done((bf16[1,64,1024]{2,1,0:T(8,128)(2,1)S(1)}, bf16[1,64,1024]{2,1,0:T(8,128)(2,1)}, u32[]{:S(2)}) %copy-start.4) | copy-done | bytes 131096
  6.8 14.9 %gather_panels.1 = (bf16[64,512]{1,0:T(8,128)(2,1)S(1)}, bf16[3,64,512]{2,1,0:T(8,128)(2,1)S(1)}, f32[3,64,128]{2,1,0:T(8,128)S(1)}, f32[3,40,128]{2,1,0:T(8,128)S(1)}, bf16[8,64,128]{2,1,0:T(8,128)(2,1)S(1)}) custom-call(bf16[64,1024]{1,0:T(8,128)(2,1)S(1)} %bitcast.11, bf16[1024,512]{1,0:T(8,128)(2,1)S(1)} %copy-done, bf16[1024,512]{1,0:T(8,128)(2,1)S(1)} %copy-done.1, ...), custom_call_target="tpu_custom_call" | custom-call | tf_op jit(solution)/shard_map/gather_panels/pallas_call | solution.py:682
  21.7 0.0 copy-done.3
  21.7 0.0 copy-done.5
  21.7 0.0 copy-done.6
  21.7 9.2 %pair_grads.1 = (bf16[64,512]{1,0:T(8,128)(2,1)S(1)}, bf16[3,64,512]{2,1,0:T(8,128)(2,1)S(1)}, bf16[144,512]{1,0:T(8,128)(2,1)S(1)}) custom-call(bf16[64,512]{1,0:T(8,128)(2,1)S(1)} %get-tuple-element.22.left_ref, bf16[3,64,512]{2,1,0:T(8,128)(2,1)S(1)} %get-tuple-element.23.right_ref, f32[1,512]{1,0:T(1,128)S(1)} %bitcast.12, ...), custom_call_target="tpu_custom_call" | custom-call | tf_op jit(solution)/shard_map/pair_grads/pallas_call | solution.py:163
  31.0 0.0 copy-done.2
  31.0 47.9 %reduce_grads.1 = (f32[64,1024]{1,0:T(8,128)S(1)}, bf16[2,8,4,128,128]{4,3,2,1,0:T(8,128)(2,1)S(1)}, bf16[8,5,16,128]{3,2,1,0:T(8,128)(2,1)S(1)}) custom-call(bf16[64,512]{1,0:T(8,128)(2,1)S(1)} %get-tuple-element.26.left_ref, bf16[3,64,512]{2,1,0:T(8,128)(2,1)S(1)} %get-tuple-element.27.right_ref, bf16[8,64,128]{2,1,0:T(8,128)(2,1)S(1)} %get-tuple-element.28.emb_ref, ...), custom_call_target="tpu_custom_call" | custom-call | tf_op jit(solution)/shard_map/reduce_grads/pallas_call | solution.py:481
  78.9 2.8 %unpack_grads.1 = (f32[1024,512]{1,0:T(8,128)}, f32[1024,512]{1,0:T(8,128)}, f32[1,512]{1,0:T(1,128)}, f32[512,128]{1,0:T(8,128)}, f32[1,128]{1,0:T(1,128)}) custom-call(bf16[2,8,4,128,128]{4,3,2,1,0:T(8,128)(2,1)S(1)} %get-tuple-element.31.pieces_ref, bf16[8,5,16,128]{3,2,1,0:T(8,128)(2,1)S(1)} %get-tuple-element.32.small_ref), custom_call_target="tpu_custom_call" | custom-call | tf_op jit(solution)/shard_map/unpack_grads/pallas_call | solution.py:547
  81.8 0.7 copy.24
  (1 shorter events, 0.0 us)
Async XLA Ops:
  0.6 4.1 %copy-start = (bf16[1024,512]{1,0:T(8,128)(2,1)S(1)}, bf16[1024,512]{1,0:T(8,128)(2,1)}, u32[]{:S(2)}) copy-start(bf16[1024,512]{1,0:T(8,128)(2,1)} %w_left_ref.3) | copy-start | bytes 3145732
  2.9 18.8 %copy-start.3 = (bf16[512,128]{1,0:T(8,128)(2,1)S(1)}, bf16[512,128]{1,0:T(8,128)(2,1)}, u32[]{:S(2)}) copy-start(bf16[512,128]{1,0:T(8,128)(2,1)} %middle_ref.1) | copy-start | bytes 393220
  2.9 18.8 %copy-start.5 = (f32[512]{0:T(512)S(1)}, f32[512]{0:T(512)}, u32[]{:S(2)}) copy-start(f32[512]{0:T(512)} %param.17) | copy-start | bytes 6148
  2.9 18.8 %copy-start.6 = (f32[128]{0:T(128)S(1)}, f32[128]{0:T(128)}, u32[]{:S(2)}) copy-start(f32[128]{0:T(128)} %param.19) | copy-start | bytes 1540
  4.7 1.2 %copy-start.1 = (bf16[1024,512]{1,0:T(8,128)(2,1)S(1)}, bf16[1024,512]{1,0:T(8,128)(2,1)}, u32[]{:S(2)}) copy-start(bf16[1024,512]{1,0:T(8,128)(2,1)} %w_right_ref.3) | copy-start | bytes 3145732
  5.9 0.9 %copy-start.4 = (bf16[1,64,1024]{2,1,0:T(8,128)(2,1)S(1)}, bf16[1,64,1024]{2,1,0:T(8,128)(2,1)}, u32[]{:S(2)}) copy-start(bf16[1,64,1024]{2,1,0:T(8,128)(2,1)} %param.10) | copy-start | bytes 393220
  6.8 24.1 %copy-start.2 = (bf16[1024,512]{1,0:T(8,128)(2,1)S(1)}, bf16[1024,512]{1,0:T(8,128)(2,1)}, u32[]{:S(2)}) copy-start(bf16[1024,512]{1,0:T(8,128)(2,1)} %w_right_ref.3) | copy-start | bytes 3145732
